TPU v7x, 512 devices: a whole 4x8x8 slice. The times are simulated.
512 devices in a mesh: ctx: 16 (over y, core), tp: 32 (over z, x).
Axes of the slice: x: 4, y: 8, z: 8, core: 2. Of those that a mesh axis runs over, the one named last changes fastest.
Arguments:
- queries: bfloat16 [4096, 8192], P('ctx', 'tp'), may hold values from -6 to 6
- keys: bfloat16 [4096, 8192], P('ctx', 'tp'), may hold values from -0.5 to 0.5
- values: bfloat16 [4096, 8192], P('ctx', 'tp'), may hold values from -64 to 64
- log_decay: float32 [4096, 64], P('ctx', 'tp'), may hold values from -0.8 to 0
- gate: bfloat16 [4096, 8192], P('ctx', 'tp'), may hold values from -6 to 6
- norm_gain: float32 [8192], P('tp'), may hold values from 0.1 to 1.9
- out_weight: bfloat16 [6144, 8192], P('tp'), may hold values from -0.125 to 0.125
- target: bfloat16 [4096, 6144], P('ctx', 'tp'), may hold values from -3 to 3
Outputs:
- output: bfloat16 [4096, 6144], P('ctx', 'tp')
- query_grad: bfloat16 [4096, 8192], P('ctx', 'tp')
- key_grad: bfloat16 [4096, 8192], P('ctx', 'tp')
- value_grad: bfloat16 [4096, 8192], P('ctx', 'tp')
- gate_grad: bfloat16 [4096, 8192], P('ctx', 'tp')
All inputs are finite; a program needn't handle non-finite values.
Results may differ from a plain program's by a relative error of at most 0.03.
Values may be sent and summed in bfloat16 or wider, within the bound.
A program may use at most 64 MiB of HBM per device.

v0:
```python
import jax
import jax.numpy as jnp
from jax import lax
from jax.sharding import PartitionSpec as P

HEAD_TOTAL = 64
DH = 128


EPS = 1e-06


def prefix(value, axis, join, neutral, backward):
    count = lax.axis_size(axis)
    place = lax.axis_index(axis)
    ahead = count - 1 - place if backward else place
    gathered = jax.tree.map(
        lambda a, kind: lax.all_gather(a.astype(kind), axis), value, (jnp.bfloat16, jnp.bfloat16)
    )
    state = jax.tree.map(lambda a, e: jnp.zeros_like(a) + jnp.asarray(e, a.dtype), value, neutral)

    def one(turn, state):
        source = count - 1 - turn if backward else turn
        return join(
            state,
            jax.tree.map(
                lambda a, own: lax.dynamic_index_in_dim(a, source, 0, False).astype(own.dtype),
                gathered,
                value,
            ),
        )

    return lax.fori_loop(0, ahead, one, state)


def decay_tables(log_block):
    cum_decay = jnp.cumsum(log_block, axis=0)
    block_total = cum_decay[-1]
    by_head = cum_decay.T
    gaps = by_head[:, :, None] - by_head[:, None, :]
    length = log_block.shape[0]
    causal = jnp.arange(length)[:, None] >= jnp.arange(length)[None, :]
    weight = jnp.where(causal[None], jnp.exp(jnp.minimum(gaps, 0.0)), 0.0)
    return (cum_decay, block_total, weight)


def combine_states(earlier, later):
    return (earlier[0] + later[0], jnp.exp(later[0])[..., None, None] * earlier[1] + later[1])


def on_device(queries, keys, values, log_decay, gate, norm_gain, out_weight, target):
    row_count = queries.shape[0]
    head_count = log_decay.shape[1]
    feature_count = head_count * DH
    query_heads = queries.reshape(row_count, head_count, DH)
    key_heads = keys.reshape(row_count, head_count, DH)
    value_heads = values.reshape(row_count, head_count, DH)
    cum_decay, block_total, weight = decay_tables(log_decay)
    scores = jnp.einsum("thd,shd->hts", query_heads, key_heads, preferred_element_type=jnp.float32)
    probs = (scores * weight).astype(jnp.bfloat16)
    decayed_keys = (key_heads * jnp.exp(block_total[None] - cum_decay)[:, :, None]).astype(
        jnp.bfloat16
    )
    own_state = jnp.einsum(
        "thd,the->hde", decayed_keys, value_heads, preferred_element_type=jnp.float32
    )
    within_block = jnp.einsum(
        "hts,she->the", probs, value_heads, preferred_element_type=jnp.float32
    )
    identity = (jnp.zeros_like(block_total), jnp.zeros_like(own_state))
    carried = prefix((block_total, own_state), "ctx", combine_states, identity, False)[1]
    state_half = carried.astype(jnp.bfloat16)
    from_state = (
        jnp.einsum("thd,hde->the", query_heads, state_half, preferred_element_type=jnp.float32)
        * jnp.exp(cum_decay)[:, :, None]
    )
    attended = (within_block + from_state).reshape(row_count, feature_count)
    square_total = lax.psum(jnp.sum(attended * attended, axis=1), "tp")
    inv_rms = lax.rsqrt(square_total[:, None] / (HEAD_TOTAL * DH) + EPS)
    gate_open = jax.nn.sigmoid(gate.astype(jnp.float32))
    normed = (attended * inv_rms * norm_gain[None] * gate_open).astype(jnp.bfloat16)
    weight_block = out_weight
    output = lax.dot_general(
        lax.all_gather(normed, "tp", axis=1, tiled=True),
        weight_block,
        (((1,), (1,)), ((), ())),
        preferred_element_type=jnp.float32,
    ).astype(jnp.bfloat16)
    output_grad = (output.astype(jnp.float32) - target.astype(jnp.float32)).astype(jnp.bfloat16)
    weight_block = out_weight
    grad_columns = lax.psum_scatter(
        lax.dot_general(
            weight_block, output_grad, (((0,), (1,)), ((), ())), preferred_element_type=jnp.float32
        ).astype(jnp.bfloat16),
        "tp",
        scatter_dimension=0,
        tiled=True,
    ).astype(jnp.float32)
    feature_grad = grad_columns.T
    gate_grad = (
        feature_grad * attended * inv_rms * norm_gain[None] * gate_open * (1.0 - gate_open)
    ).astype(jnp.bfloat16)
    normed_grad = feature_grad * norm_gain[None] * gate_open
    product_total = lax.psum(jnp.sum(normed_grad * attended, axis=1), "tp")
    mean_product = product_total[:, None] / (HEAD_TOTAL * DH)
    attn_grad = (inv_rms * normed_grad - inv_rms**3 * attended * mean_product).astype(jnp.bfloat16)
    grad_heads = attn_grad.reshape(row_count, head_count, DH)
    decayed_queries = (query_heads * jnp.exp(cum_decay)[:, :, None]).astype(jnp.bfloat16)
    own_grad = jnp.einsum(
        "thd,the->hde", decayed_queries, grad_heads, preferred_element_type=jnp.float32
    )
    value_scores = jnp.einsum(
        "the,she->hts", grad_heads, value_heads, preferred_element_type=jnp.float32
    )
    score_grad = (value_scores * weight).astype(jnp.bfloat16)
    query_local = jnp.einsum(
        "hts,shd->thd", score_grad, key_heads, preferred_element_type=jnp.float32
    )
    key_local = jnp.einsum(
        "hts,thd->shd", score_grad, query_heads, preferred_element_type=jnp.float32
    )
    value_local = jnp.einsum("hts,the->she", probs, grad_heads, preferred_element_type=jnp.float32)
    identity = (jnp.zeros_like(block_total), jnp.zeros_like(own_grad))
    grad_carried = prefix((block_total, own_grad), "ctx", combine_states, identity, True)[1]
    grad_half = grad_carried.astype(jnp.bfloat16)
    query_grad = query_local + jnp.exp(cum_decay)[:, :, None] * jnp.einsum(
        "the,hde->thd", grad_heads, state_half, preferred_element_type=jnp.float32
    )
    key_grad = key_local + jnp.exp(block_total[None] - cum_decay)[:, :, None] * jnp.einsum(
        "she,hde->shd", value_heads, grad_half, preferred_element_type=jnp.float32
    )
    value_grad = value_local + jnp.einsum(
        "shd,hde->she", decayed_keys, grad_half, preferred_element_type=jnp.float32
    )
    return (
        output,
        query_grad.reshape(row_count, feature_count).astype(jnp.bfloat16),
        key_grad.reshape(row_count, feature_count).astype(jnp.bfloat16),
        value_grad.reshape(row_count, feature_count).astype(jnp.bfloat16),
        gate_grad,
    )


def solution(mesh):
    return jax.shard_map(
        on_device,
        mesh=mesh,
        in_specs=(
            P("ctx", "tp"),
            P("ctx", "tp"),
            P("ctx", "tp"),
            P("ctx", "tp"),
            P("ctx", "tp"),
            P("tp"),
            P("tp", None),
            P("ctx", "tp"),
        ),
        out_specs=(P("ctx", "tp"), P("ctx", "tp"), P("ctx", "tp"), P("ctx", "tp"), P("ctx", "tp")),
        check_vma=False,
    )
```

profile of v0, /device:TPU:1, one launch (start us, length us, event | category | flops | bytes accessed | tf_op | source)
XLA Modules:
  0.0 626.2 jit_solution(10710695476704481782)
XLA Ops:
  9.4 1.0 copy.127
  10.4 1.8 convolution_convert_fusion.3
  12.4 20.7 %all-gather.2 = bf16[16,1,2]{2,1,0:T(2,128)(2,1)S(1)} all-gather(bf16[1,1,2]{2,1,0:T(2,128)(2,1)S(1)} %bitcast.162), channel_id=1, replica_groups=mesh['ctx'=16,'tp'=32] {'ctx'}, dimensions={0}, use_global_device_ids=true | all-gather | bytes 68 | tf_op jit(solution)/shard_map/all_gather | solution.py:18
  33.4 1.0 copy.126
  35.1 1.7 fusion.1
  36.8 22.3 %all-gather.9.cloned.1.call-done = bf16[32,128,128]{2,1,0:T(8,128)(2,1)} async-done(((bf16[2,128,128]{2,1,0:T(8,128)(2,1)}), bf16[32,128,128]{2,1,0:T(8,128)(2,1)}) %all-gather.9.cloned.1.call-update) | async-done | bytes 1048592 | tf_op jit(solution)/shard_map/all_gather | solution.py:18
  59.1 1.0 while.26
  59.1 0.9 convert_add_fusion.4
  60.3 2.4 multiply_reduce_fusion.1
  62.8 1.1 copy.136
  63.9 62.5 %psum.14 = f32[256]{0:T(256)} all-reduce(f32[256]{0:T(256)} %get-tuple-element.238), channel_id=1, replica_groups=mesh['ctx'=16,'tp'=32] {'tp'}, use_global_device_ids=true, to_apply=%region_5.6 | all-reduce | flops 256 | bytes 2048 | tf_op jit(solution)/shard_map/psum | solution.py:78
  126.3 1.2 multiply_multiply_fusion
  127.5 1.7 multiply_convert_fusion.1
  129.3 104.1 %all-gather.7.cloned.1.call-done = bf16[256,8192]{1,0:T(8,128)(2,1)} async-done(((bf16[256,256]{1,0:T(8,128)(2,1)}), bf16[256,8192]{1,0:T(8,128)(2,1)}) %all-gather.7.cloned.1.call-update) | async-done | bytes 4194320 | tf_op jit(solution)/shard_map/all_gather | solution.py:84
  233.4 3.8 convolution_convert_fusion.1
  237.8 3.2 fusion
  241.1 226.5 %reduce-scatter.2.cloned.1.call-done = bf16[256,256]{0,1:T(8,128)(2,1)} async-done(((bf16[8192,256]{0,1:T(8,128)(2,1)}), bf16[256,256]{0,1:T(8,128)(2,1)}) %reduce-scatter.2.cloned.1.call-update) | async-done | bytes 131088 | tf_op jit(solution)/shard_map/reduce_scatter | solution.py:91
  467.6 1.7 multiply_reduce_fusion
  469.3 59.5 %psum.15 = f32[256]{0:T(256)} all-reduce(f32[256]{0:T(256)} %multiply_reduce_fusion), channel_id=1, replica_groups=mesh['ctx'=16,'tp'=32] {'tp'}, use_global_device_ids=true, to_apply=%region_8.9 | all-reduce | flops 256 | bytes 2048 | tf_op jit(solution)/shard_map/psum | solution.py:104
  529.4 1.8 fusion.17
  531.3 1.0 copy.158
  532.3 1.7 convolution_convert_fusion.2
  534.2 1.2 fusion.2
  536.2 1.1 fusion.9
  538.1 1.9 fusion.33
  539.9 51.0 %all-gather.11.cloned.1.call-done = bf16[32,128,128]{2,1,0:T(8,128)(2,1)} async-done(((bf16[2,128,128]{2,1,0:T(8,128)(2,1)}), bf16[32,128,128]{2,1,0:T(8,128)(2,1)}) %all-gather.11.cloned.1.call-update) | async-done | bytes 1048592 | tf_op jit(solution)/shard_map/all_gather | solution.py:18
  590.9 23.0 %while.27 = (s32[]{:T(128)}, f32[2,128,128]{2,1,0:T(8,128)S(1)}, s32[]{:T(128)}, bf16[16,2]{1,0:T(8,128)(2,1)}, bf16[16,2,128,128]{3,2,1,0:T(8,128)(2,1)}, /*index=5*/s32[]{:T(128)}, s32[]{:T(128)}, s32[]{:T(128)}, s32[]{:T(128)}) while((s32[]{:T(128)}, f32[2,128,128]{2,1,0:T(8,128)S(1)}, s32[]{:T(128)}, bf16[16,2]{1,0:T(8,128)(2,1)}, ...), condition=%wide.region_10.11_spmd, body=%wide.region_9.10_spmd.sunk | while | flops 98312 | bytes 327847 | solution.py:33
  591.6 0.9 convert_add_fusion.5
  593.2 0.9 convert_add_fusion.5
  613.9 1.8 fusion.6
  615.7 1.2 fusion.10
  617.7 1.2 fusion.11
  (79 shorter events, 28.9 us)
Async XLA Ops:
  7.2 226.2 %copy-start = (bf16[192,8192]{1,0:T(8,128)(2,1)S(1)}, bf16[192,8192]{1,0:T(8,128)(2,1)}, u32[]{:S(2)}) copy-start(bf16[192,8192]{1,0:T(8,128)(2,1)} %param.18) | copy-start | bytes 9437188
  7.2 53.1 %copy-start.5 = (bf16[256,256]{1,0:T(8,128)(2,1)S(1)}, bf16[256,256]{1,0:T(8,128)(2,1)}, u32[]{:S(2)}) copy-start(bf16[256,256]{1,0:T(8,128)(2,1)} %param.14) | copy-start | bytes 393220
  7.2 120.3 %copy-start.9 = (f32[256]{0:T(256)S(1)}, f32[256]{0:T(256)}, u32[]{:S(2)}) copy-start(f32[256]{0:T(256)} %param.17) | copy-start | bytes 3076
  7.2 51.9 %all-gather.9.cloned.1.call-start = ((), (), s32[]{:S(2)}) async-start(), calls=%async_computation.3 | async-start | bytes 1114112 | tf_op jit(solution)/shard_map/all_gather | solution.py:18
  9.1 3.3 copy-start.11
  10.4 48.7 %copy-start.3 = (bf16[256,256]{0,1:T(8,128)(2,1)}, bf16[256,256]{0,1:T(8,128)(2,1)S(1)}, u32[]{:S(2)}) copy-start(bf16[256,256]{0,1:T(8,128)(2,1)S(1)} %copy.127) | copy-start | bytes 393220
  12.2 221.2 %all-gather.7.cloned.1.call-start = ((), (), s32[]{:S(2)}) async-start(), calls=%async_computation.1 | async-start | bytes 4325376 | tf_op jit(solution)/shard_map/all_gather | solution.py:84
  34.4 28.4 %copy-start.1 = (bf16[256,256]{0,1:T(8,128)(2,1)}, bf16[256,256]{0,1:T(8,128)(2,1)S(1)}, u32[]{:S(2)}) copy-start(bf16[256,256]{0,1:T(8,128)(2,1)S(1)} %copy.126) | copy-start | bytes 393220
  34.4 0.7 copy-start.8
  60.1 3.8 copy-start.10
  129.2 338.4 %reduce-scatter.2.cloned.1.call-start = ((), (), s32[]{:S(2)}) async-start(), calls=%async_computation.2 | async-start | bytes 4325376 | tf_op jit(solution)/shard_map/reduce_scatter | solution.py:91
  233.4 4.4 copy-start.7
  237.1 0.6 copy-start.6
  241.0 349.9 %all-gather.11.cloned.1.call-start = ((), (), s32[]{:S(2)}) async-start(), calls=%async_computation.4 | async-start | bytes 1114112 | tf_op jit(solution)/shard_map/all_gather | solution.py:18
  531.3 86.4 %copy-start.2 = (bf16[256,256]{0,1:T(8,128)(2,1)S(1)}, bf16[256,256]{0,1:T(8,128)(2,1)}, u32[]{:S(2)}) copy-start(bf16[256,256]{0,1:T(8,128)(2,1)} %copy-done.1) | copy-start | bytes 393220
  535.4 0.7 copy-start.4
Sparse Core Ops, SparseCore 0:
  12.3 46.6 all-gather.8
  129.3 103.9 all-gather.6
  241.1 226.4 reduce-scatter.1
  534.2 56.6 all-gather.10
where the time goes:
time: 628 us; the launch traced here: 626 us
  waiting for transfers between devices  404 us (64%)
  blocking collectives  143 us (23%)
  other arithmetic  31.6 us (5%)
  matrix products  23.4 us (4%)
  between operations  14 us (2%)
  local copies, waits for them, and re-layouts  10 us (2%)
    reduce_scatter x1, waiting for transfers between devices, on_device(): lax.psum_scatter(lax.dot_general(weight_block, output_grad, (((0,), (1,))...  227 us
    all_gather x1, waiting for transfers between devices, on_device(): lax.all_gather(normed, 'tp', axis=1, tiled=True)  104 us
    all_gather x2, waiting for transfers between devices, prefix(): lax.all_gather(a.astype(kind), axis)  73.2 us
    psum x1, blocking collectives, on_device(): square_total = lax.psum(jnp.sum(attended * attended, axis=1), 'tp')  62.5 us
    psum x1, blocking collectives, on_device(): product_total = lax.psum(jnp.sum(normed_grad * attended, axis=1), 'tp')  59.5 us
    all_gather x1, blocking collectives, prefix(): lax.all_gather(a.astype(kind), axis)  20.7 us
    add x15, other arithmetic, combine_states(): jnp.exp(later[0])[..., None, None] * earlier[1] + later[1]  13.9 us
  transfers between devices with their start and end apart: 4, of which 4 were waited for; matrix products, arithmetic and copies ran while one was open for 1% of the time, Pallas kernels for 0%

commit v1 on v0

v1 whole, which is shorter than its diff:
```python
import functools

import jax
import jax.numpy as jnp
from jax import lax
from jax.experimental import pallas as pl
from jax.experimental.pallas import tpu as pltpu
from jax.sharding import PartitionSpec as P

DH = 128
EPS = 1e-06
MESH = pl.DeviceIdType.MESH
F32 = jnp.float32
BF16 = jnp.bfloat16
X = 4


def nn(a, b):
    return lax.dot_general(a, b, (((1,), (0,)), ((), ())), preferred_element_type=F32)


def nt(a, b):
    return lax.dot_general(a, b, (((1,), (1,)), ((), ())), preferred_element_type=F32)


def tn(a, b):
    return lax.dot_general(a, b, (((0,), (0,)), ((), ())), preferred_element_type=F32)


def identity(size):
    row = lax.broadcasted_iota(jnp.int32, (size, size), 0)
    column = lax.broadcasted_iota(jnp.int32, (size, size), 1)
    return jnp.where(row == column, 1.0, 0.0).astype(BF16)


def as_row(column):
    return jnp.broadcast_to(column, (column.shape[0], 128)).T[0:1, :]


def as_columns(row):
    return jnp.broadcast_to(row, (128, row.shape[1])).T


def kernel(
    sizes,
    q_ref,
    k_ref,
    v_ref,
    ld_ref,
    gate_ref,
    gain_ref,
    w_ref,
    target_ref,
    out_ref,
    qg_ref,
    kg_ref,
    vg_ref,
    gg_ref,
    wb,
    wrelay,
    uall,
    yacc,
    ystage,
    yrecv,
    gx,
    gall,
    fstage,
    frecv,
    weight,
    probs,
    kdec,
    att,
    klocal,
    vlocal,
    targett,
    agrad,
    bown,
    bsib,
    bchip,
    s_out,
    s_in,
    s_keep,
    t_out,
    t_in,
    c_acc,
    d_acc,
    c_out,
    state,
    small_z,
    small_x,
    w_send,
    w_recv,
    w_own,
    ws_send,
    ws_recv,
    u_send,
    u_recv,
    y_send,
    y_recv,
    g_send,
    g_recv,
    f_send,
    f_recv,
    b_send,
    b_recv,
    bc_send,
    bc_recv,
    s_send,
    s_recv,
    t_send,
    t_recv,
    c_send,
    c_recv,
    sz_send,
    sz_recv,
    sx_send,
    sx_recv,
):
    Y, Z = sizes
    tokens = q_ref.shape[0]
    half_tokens = tokens // 2
    rows = w_ref.shape[0]
    half = rows // 2
    width = q_ref.shape[1]
    total_features = w_ref.shape[1]
    heads = width // DH

    ctx = lax.axis_index("ctx")
    tp = lax.axis_index("tp")
    core = lax.rem(ctx, 2)
    y = lax.div(ctx, 2)
    x = lax.rem(tp, X)
    z = lax.div(tp, X)
    sibling = (y * 2 + 1 - core, tp)
    is_zero = core == 0

    def xs(step):
        return lax.rem(x + step + X, X)

    def zs(step):
        return lax.rem(z + step + 2 * Z, Z)

    def at_x(step):
        return (ctx, z * X + xs(step))

    def at_z(step):
        return (ctx, zs(step) * X + x)

    def at_y(place):
        return (place * 2 + core, tp)

    sign = 1 - 2 * core
    left, right, opp = xs(-1), xs(1), xs(2)

    def send(src, dst, send_sem, recv_sem, device):
        copy = pltpu.make_async_remote_copy(
            src_ref=src,
            dst_ref=dst,
            send_sem=send_sem,
            recv_sem=recv_sem,
            device_id=device,
            device_id_type=MESH,
        )
        copy.start()

    def arrived(ref, sem):
        pltpu.make_async_copy(ref, ref, sem).wait()

    barrier = pltpu.get_barrier_semaphore()
    partners = [sibling] + [at_x(step) for step in range(1, X)]
    partners += [at_z(step) for step in range(1, Z)]
    partners += [at_y(lax.rem(y + step, Y)) for step in range(1, Y)]
    for partner in partners:
        pl.semaphore_signal(barrier, inc=1, device_id=partner, device_id_type=MESH)
    pl.semaphore_wait(barrier, len(partners))

    def w_columns(block, x_to):
        start = pl.multiple_of((block * X + x_to) * width, width)
        return pl.ds(start, width)

    my_rows = pl.ds(pl.multiple_of(core * half, half), half)
    x_far = xs(sign)

    def w_far(block, carry):
        send(w_ref.at[my_rows, w_columns(block, opp)], wrelay.at[block], w_send.at[0], w_recv.at[0], (ctx, z * X + x_far))
        return carry

    def w_near(block, carry):
        send(w_ref.at[my_rows, w_columns(block, right)], wb.at[block, x, core], w_send.at[1], w_recv.at[1], at_x(1))
        send(w_ref.at[my_rows, w_columns(block, left)], wb.at[block, x, core], w_send.at[2], w_recv.at[2], at_x(-1))
        return carry

    def w_mine(block, carry):
        for part in range(2):
            pltpu.make_async_copy(
                w_ref.at[pl.ds(part * half, half), w_columns(block, x)], wb.at[block, x, part], w_own
            ).start()
        return carry

    lax.fori_loop(0, Z, w_far, 0)
    lax.fori_loop(0, Z, w_near, 0)
    lax.fori_loop(0, Z, w_mine, 0)

    row = lax.broadcasted_iota(jnp.int32, (tokens, tokens), 0)
    column = lax.broadcasted_iota(jnp.int32, (tokens, tokens), 1)
    causal = row >= column
    cum = lax.dot_general(
        jnp.where(causal, 1.0, 0.0).astype(F32),
        ld_ref[...],
        (((1,), (0,)), ((), ())),
        precision=lax.Precision.HIGHEST,
        preferred_element_type=F32,
    )
    cums = [cum[:, h : h + 1] for h in range(heads)]
    totals = [c[tokens - 1 : tokens, :] for c in cums]
    bown[...] = jnp.zeros_like(bown)
    for h in range(heads):
        bown[h : h + 1, :] = jnp.broadcast_to(totals[h], (1, 128))
    send(bown, bsib, b_send, b_recv, sibling)

    def lanes(h):
        return slice(h * DH, (h + 1) * DH)

    own = []
    for h in range(heads):
        decayed = (k_ref[:, lanes(h)].astype(F32) * jnp.exp(totals[h] - cums[h])).astype(BF16)
        kdec[:, lanes(h)] = decayed
        own.append(tn(decayed, v_ref[:, lanes(h)]))

    def of_core(pair):
        return jnp.where(is_zero, pair[0], pair[1])

    def scan_share(turn, states):
        s_out[turn] = of_core((states[1], states[0])).astype(BF16)
        s_keep[turn] = of_core((states[0], states[1]))
        send(s_out.at[turn], s_in.at[turn], s_send.at[turn], s_recv.at[turn], sibling)

    def scan_way(turn):
        step = 1 if turn == 0 else -1
        first_here = is_zero if turn == 0 else jnp.logical_not(is_zero)
        return step, first_here

    def decays(ref):
        return of_core((ref[0:1, :], ref[1:2, :]))

    def reaches(place):
        return jnp.logical_and(place >= 0, place < Y)

    def scan_send(turn):
        step, first_here = scan_way(turn)
        arrived(s_in.at[turn], s_recv.at[turn])
        mine = s_keep[turn]
        theirs = s_in[turn].astype(F32)
        first = jnp.where(first_here, mine, theirs)
        second = jnp.where(first_here, theirs, mine)
        s_keep[turn] = first
        b_second = jnp.where(first_here, decays(bsib), decays(bown))
        t_out[turn] = (jnp.exp(b_second) * first + second).astype(BF16)
        for distance in range(1, Y):
            place = y + step * distance

            @pl.when(reaches(place))
            def _():
                send(
                    t_out.at[turn],
                    t_in.at[turn, distance - 1],
                    t_send.at[turn, distance - 1],
                    t_recv.at[turn, distance - 1],
                    at_y(place),
                )

    def scan_end(turn):
        step, first_here = scan_way(turn)
        c_acc[...] = jnp.zeros_like(c_acc)
        d_acc[...] = jnp.zeros_like(d_acc)
        for distance in range(1, Y):
            place = y - step * distance

            @pl.when(reaches(place))
            def _():
                slot = t_in.at[turn, distance - 1]
                arrived(slot, t_recv.at[turn, distance - 1])
                between = d_acc[0:1, :]
                c_acc[...] += jnp.exp(between) * slot[...].astype(F32)
                d_acc[0:1, :] = between + decays(bchip.at[place])

        b_first = jnp.where(first_here, decays(bown), decays(bsib))
        carried = c_acc[...]
        after = jnp.exp(b_first) * carried + s_keep[turn]
        state[turn, core] = jnp.where(first_here, carried, after).astype(BF16)
        c_out[turn] = jnp.where(first_here, after, carried).astype(BF16)
        send(c_out.at[turn], state.at[turn, core], c_send.at[turn], c_recv.at[turn], sibling)
        arrived(c_out.at[turn], c_recv.at[turn])

    scan_share(0, own)

    arrived(bsib, b_recv)
    bchip[y] = bown[...] + bsib[...]
    for distance in range(1, Y):
        place = lax.rem(y + distance, Y)
        send(bchip.at[y], bchip.at[y], bc_send.at[distance - 1], bc_recv.at[distance - 1], at_y(place))
    scan_send(0)

    for h in range(heads):
        gaps = cums[h] - as_row(cums[h])
        decay = jnp.where(causal, jnp.exp(jnp.minimum(gaps, 0.0)), 0.0)
        weight[h] = decay
        probs[h] = (nt(q_ref[:, lanes(h)], k_ref[:, lanes(h)]) * decay).astype(BF16)
        att[:, lanes(h)] = nn(probs[h], v_ref[:, lanes(h)])
    targett[...] = nt(identity(rows), target_ref[...])

    for distance in range(1, Y):
        arrived(bchip.at[lax.rem(y - distance + Y, Y)], bc_recv.at[distance - 1])

    arrived(wrelay, w_recv.at[0])
    send(wrelay, wb.at[:, xs(-sign), core], w_send.at[3], w_recv.at[3], (ctx, z * X + x_far))

    scan_end(0)

    gain = gain_ref[...]
    squares = jnp.zeros((tokens, 1), F32)
    for h in range(heads):
        from_state = nn(q_ref[:, lanes(h)], state[0, h]) * jnp.exp(cums[h])
        attended = att[:, lanes(h)] + from_state
        att[:, lanes(h)] = attended
        squares = squares + jnp.sum(attended * attended, axis=1, keepdims=True)
        gate_open = jax.nn.sigmoid(gate_ref[:, lanes(h)].astype(F32))
        uall[z, :, lanes(h)] = (attended * gain[:, lanes(h)] * gate_open).astype(BF16)

    far, near = Z // 2, Z - 1 - Z // 2
    hops = (far, near)
    ways = (sign, -sign)

    def u_part(way, step, part):
        return uall.at[zs(-ways[way] * step), pl.ds(part * half_tokens, half_tokens)]

    def u_start(way, step, part):
        ref = u_part(way, step, part)
        send(ref, ref, u_send.at[way, step, part], u_recv.at[way, step, part], at_z(ways[way]))

    for part in range(2):
        for way in range(2):
            if hops[way] > 0:
                u_start(way, 0, part)

    def small_share(turn, value):
        small_z[turn, 0] = value
        for step in range(1, Z):
            send(small_z.at[turn, 0], small_z.at[turn, step], sz_send.at[turn, step - 1], sz_recv.at[turn, step - 1], at_z(step))

    def small_cross(turn):
        for step in range(1, Z):
            arrived(small_z.at[turn, step], sz_recv.at[turn, step - 1])
        sum_z = small_z[turn, 0]
        for step in range(1, Z):
            sum_z = sum_z + small_z[turn, step]
        small_x[turn, 0] = sum_z
        for step in range(1, X):
            send(small_x.at[turn, 0], small_x.at[turn, step], sx_send.at[turn, step - 1], sx_recv.at[turn, step - 1], at_x(step))

    def small_sum(turn):
        for step in range(1, X):
            arrived(small_x.at[turn, step], sx_recv.at[turn, step - 1])
        sum_x = small_x[turn, 0]
        for step in range(1, X):
            sum_x = sum_x + small_x[turn, step]
        return sum_x

    small_share(0, as_row(squares))

    def w_pair(source, sem, slot):
        ref = wb.at[:, source, core]
        arrived(ref, sem)
        send(ref, ref, ws_send.at[slot], ws_recv.at[slot], sibling)

    w_pair(left, w_recv.at[1], 0)
    w_pair(right, w_recv.at[2], 1)
    w_pair(opp, w_recv.at[3], 2)
    for part in range(2):
        arrived(wb.at[:, x, part], w_own)
    for slot, source in enumerate((left, right, opp)):
        arrived(wb.at[:, source, 1 - core], ws_recv.at[slot])

    def w_block(block):
        return wb[block].reshape(X * rows, width)

    yacc[...] = nt(w_block(z), uall[z]).reshape(yacc.shape)

    def accumulate(block):
        yacc[...] += nt(w_block(block), uall[block]).reshape(yacc.shape)

    for step in range(far):
        for part in range(2):
            for way in range(2):
                if step < hops[way]:
                    arrived(u_part(way, step + 1, part), u_recv.at[way, step, part])
                    if step + 1 < hops[way]:
                        u_start(way, step + 1, part)
        for way in range(2):
            if step < hops[way]:
                accumulate(zs(-ways[way] * (step + 1)))

    small_cross(0)

    def y_start(kind, part, value, device):
        ystage[kind, part] = value.astype(BF16)
        send(ystage.at[kind, part], yrecv.at[kind, part], y_send.at[kind, part], y_recv.at[kind, part], device)

    y_start(0, 0, yacc[opp, 0], at_x(1))
    y_start(0, 1, yacc[opp, 1], at_x(-1))
    y_start(1, 1, yacc[right, 1], at_x(1))
    y_start(1, 0, yacc[left, 0], at_x(-1))
    arrived(yrecv.at[0, 0], y_recv.at[0, 0])
    y_start(2, 0, yacc[right, 0] + yrecv[0, 0].astype(F32), at_x(1))
    arrived(yrecv.at[0, 1], y_recv.at[0, 1])
    y_start(2, 1, yacc[left, 1] + yrecv[0, 1].astype(F32), at_x(-1))

    mean_square = small_sum(0) / total_features
    inv_rms = lax.rsqrt(mean_square + EPS)

    product = jnp.zeros((1, tokens), F32)
    outs = []
    for part in range(2):
        for kind in (1, 2):
            arrived(yrecv.at[kind, part], y_recv.at[kind, part])
        total = yacc[x, part] + yrecv[1, part].astype(F32) + yrecv[2, part].astype(F32)
        out_half = (total * inv_rms).astype(BF16)
        grad = (out_half.astype(F32) - targett[part * half : (part + 1) * half, :]).astype(BF16)
        gx[x, part] = grad
        outs.append(out_half)
        product = product + jnp.sum(grad.astype(F32) * total, axis=0, keepdims=True)

    def g_start(source, part, kind, device):
        ref = gx.at[source, part]
        send(ref, ref, g_send.at[kind, part], g_recv.at[kind, part], device)

    g_start(x, 0, 0, at_x(1))
    g_start(x, 1, 1, at_x(-1))
    g_start(x, 1, 0, at_x(1))
    g_start(x, 0, 1, at_x(-1))
    small_share(1, product)
    eye = identity(tokens)
    out_ref[...] = nt(eye, jnp.concatenate(outs, axis=0)).astype(BF16)
    arrived(gx.at[left, 0], g_recv.at[0, 0])
    g_start(left, 0, 2, at_x(1))
    arrived(gx.at[right, 1], g_recv.at[1, 1])
    g_start(right, 1, 2, at_x(-1))
    arrived(gx.at[left, 1], g_recv.at[0, 1])
    arrived(gx.at[right, 0], g_recv.at[1, 0])
    small_cross(1)
    for part in range(2):
        arrived(gx.at[opp, part], g_recv.at[2, part])
    gall[...] = nt(eye, gx[...].reshape(X * rows, tokens)).astype(BF16)

    def feature_part(block):
        return nn(gall[...], w_block(block))

    def f_slot(way, step):
        return way * far + step

    def f_start(way, step, part, value):
        piece = pl.ds(part * half_tokens, half_tokens)
        slot = f_slot(way, step)
        fstage[slot, piece] = value.astype(BF16)
        send(fstage.at[slot, piece], frecv.at[slot, piece], f_send.at[slot, part], f_recv.at[slot, part], at_z(ways[way]))

    def f_arrived(way, step, part):
        piece = pl.ds(part * half_tokens, half_tokens)
        slot = f_slot(way, step)
        arrived(frecv.at[slot, piece], f_recv.at[slot, part])
        return frecv[slot, piece].astype(F32)

    for step in range(far):
        sums = [feature_part(zs(ways[way] * (hops[way] - step))) if step < hops[way] else None for way in range(2)]
        for part in range(2):
            for way in range(2):
                if step < hops[way]:
                    value = sums[way][part * half_tokens : (part + 1) * half_tokens, :]
                    if step > 0:
                        value = value + f_arrived(way, step - 1, part)
                    f_start(way, step, part, value)

    own_feature = feature_part(z)
    mean_product = small_sum(1) / total_features
    inv = as_columns(inv_rms)
    mean_product = as_columns(mean_product)
    feature = []
    for part in range(2):
        value = own_feature[part * half_tokens : (part + 1) * half_tokens, :]
        for way in range(2):
            if hops[way] > 0:
                value = value + f_arrived(way, hops[way] - 1, part)
        feature.append(value)
    feature_grad = jnp.concatenate(feature, axis=0)

    own = []
    for h in range(heads):
        attended = att[:, lanes(h)]
        gate_open = jax.nn.sigmoid(gate_ref[:, lanes(h)].astype(F32))
        normed_grad = feature_grad[:, lanes(h)] * gain[:, lanes(h)] * gate_open
        gg_ref[:, lanes(h)] = (normed_grad * attended * inv * (1.0 - gate_open)).astype(BF16)
        grad = (inv * normed_grad - inv * inv * inv * attended * mean_product).astype(BF16)
        agrad[:, lanes(h)] = grad
        decayed = (q_ref[:, lanes(h)].astype(F32) * jnp.exp(cums[h])).astype(BF16)
        own.append(tn(decayed, grad))

    scan_share(1, own)
    for h in range(heads):
        grad = agrad[:, lanes(h)]
        score_grad = (nt(grad, v_ref[:, lanes(h)]) * weight[h]).astype(BF16)
        if h == 0:
            scan_send(1)
        qg_ref[:, lanes(h)] = (
            nn(score_grad, k_ref[:, lanes(h)]) + jnp.exp(cums[h]) * nt(grad, state[0, h])
        ).astype(BF16)
        klocal[:, lanes(h)] = tn(score_grad, q_ref[:, lanes(h)])
        vlocal[:, lanes(h)] = tn(probs[h], grad)
    scan_end(1)
    for h in range(heads):
        later = state[1, h]
        kg_ref[:, lanes(h)] = (
            klocal[:, lanes(h)] + jnp.exp(totals[h] - cums[h]) * nt(v_ref[:, lanes(h)], later)
        ).astype(BF16)
        vg_ref[:, lanes(h)] = (vlocal[:, lanes(h)] + nn(kdec[:, lanes(h)], later)).astype(BF16)

    for index in range(4):
        arrived(wrelay, w_send.at[index])
    for index in range(3):
        arrived(wrelay, ws_send.at[index])
    for way in range(2):
        for step in range(hops[way]):
            for part in range(2):
                arrived(u_part(way, step, part), u_send.at[way, step, part])
                arrived(u_part(way, step, part), f_send.at[f_slot(way, step), part])
    for kind in range(3):
        for part in range(2):
            arrived(ystage.at[kind, part], y_send.at[kind, part])
            arrived(ystage.at[kind, part], g_send.at[kind, part])
    arrived(bown, b_send)
    for distance in range(1, Y):
        arrived(bown, bc_send.at[distance - 1])
    for turn in range(2):
        arrived(s_out.at[turn], s_send.at[turn])
        arrived(c_out.at[turn], c_send.at[turn])
        step, _ = scan_way(turn)
        for distance in range(1, Y):

            @pl.when(reaches(y + step * distance))
            def _():
                arrived(t_out.at[turn], t_send.at[turn, distance - 1])

        for distance in range(1, Z):
            arrived(small_z.at[turn, 0], sz_send.at[turn, distance - 1])
        for distance in range(1, X):
            arrived(small_x.at[turn, 0], sx_send.at[turn, distance - 1])


def on_device(chips, queries, keys, values, log_decay, gate, norm_gain, out_weight, target):
    Y, Z = chips
    tokens, width = queries.shape
    rows, features = out_weight.shape
    half = rows // 2
    far = Z // 2
    vmem = pltpu.VMEM
    dma = pltpu.SemaphoreType.DMA
    scratch = [
        vmem((Z, X, 2, half, width), BF16),
        vmem((Z, half, width), BF16),
        vmem((Z, tokens, width), BF16),
        vmem((X, 2, half, tokens), F32),
        vmem((3, 2, half, tokens), BF16),
        vmem((3, 2, half, tokens), BF16),
        vmem((X, 2, half, tokens), BF16),
        vmem((tokens, X * rows), BF16),
        vmem((Z - 1, tokens, width), BF16),
        vmem((Z - 1, tokens, width), BF16),
        vmem((width // DH, tokens, tokens), F32),
        vmem((width // DH, tokens, tokens), BF16),
        vmem((tokens, width), BF16),
        vmem((tokens, width), F32),
        vmem((tokens, width), F32),
        vmem((tokens, width), F32),
        vmem((rows, tokens), F32),
        vmem((tokens, width), BF16),
        vmem((8, 128), F32),
        vmem((8, 128), F32),
        vmem((Y, 8, 128), F32),
        vmem((2, DH, DH), BF16),
        vmem((2, DH, DH), BF16),
        vmem((2, DH, DH), F32),
        vmem((2, DH, DH), BF16),
        vmem((2, max(Y - 1, 1), DH, DH), BF16),
        vmem((DH, DH), F32),
        vmem((8, 128), F32),
        vmem((2, DH, DH), BF16),
        vmem((2, 2, DH, DH), BF16),
        vmem((2, Z, 1, tokens), F32),
        vmem((2, X, 1, tokens), F32),
        dma((4,)),
        dma((4,)),
        dma,
        dma((3,)),
        dma((3,)),
        dma((2, far, 2)),
        dma((2, far, 2)),
        dma((3, 2)),
        dma((3, 2)),
        dma((3, 2)),
        dma((3, 2)),
        dma((Z - 1, 2)),
        dma((Z - 1, 2)),
        dma,
        dma,
        dma((max(Y - 1, 1),)),
        dma((max(Y - 1, 1),)),
        dma((2,)),
        dma((2,)),
        dma((2, max(Y - 1, 1))),
        dma((2, max(Y - 1, 1))),
        dma((2,)),
        dma((2,)),
        dma((2, Z - 1)),
        dma((2, Z - 1)),
        dma((2, X - 1)),
        dma((2, X - 1)),
    ]
    in_vmem = pl.BlockSpec(memory_space=pltpu.VMEM)
    wide = jax.ShapeDtypeStruct((tokens, width), BF16)
    return pl.pallas_call(
        functools.partial(kernel, chips),
        out_shape=(jax.ShapeDtypeStruct((tokens, rows), BF16), wide, wide, wide, wide),
        in_specs=[in_vmem] * 6 + [pl.BlockSpec(memory_space=pl.ANY), in_vmem],
        out_specs=(in_vmem,) * 5,
        scratch_shapes=scratch,
        compiler_params=pltpu.CompilerParams(
            collective_id=0, has_side_effects=True, vmem_limit_bytes=48 * 1024 * 1024
        ),
        cost_estimate=pl.CostEstimate(flops=2 * 10**9, bytes_accessed=8 * 10**6, transcendentals=10**6),
        name="attention_layer",
    )(queries, keys, values, log_decay, gate, norm_gain.reshape(1, width), out_weight, target)


def solution(mesh):
    chips = (mesh.shape["ctx"] // 2, mesh.shape["tp"] // X)
    return jax.shard_map(
        functools.partial(on_device, chips),
        mesh=mesh,
        in_specs=(
            P("ctx", "tp"),
            P("ctx", "tp"),
            P("ctx", "tp"),
            P("ctx", "tp"),
            P("ctx", "tp"),
            P("tp"),
            P("tp", None),
            P("ctx", "tp"),
        ),
        out_specs=(P("ctx", "tp"),) * 5,
        check_vma=False,
    )
```

time: 628 us -> 103 us (0.16)
  waiting for transfers between devices: 404 us -> 0 us
  blocking collectives: 143 us -> 0 us
  Pallas kernels: 0 us -> 89.9 us
  other arithmetic: 31.6 us -> 0 us
  matrix products: 23.4 us -> 0 us
  between operations: 14 us -> 0.67 us
    reduce_scatter x1 -> x0, waiting for transfers between devices: 227 us -> none  [on_device(): lax.psum_scatter(lax.dot_general(weight_block, output_grad, (((0,), (1,))...]
    all_gather x3 -> x0, waiting for transfers between devices: 177 us -> none  [the longest x1 104 us: on_device(): lax.all_gather(normed, 'tp', axis=1, tiled=True)]
    psum x2 -> x0, blocking collectives: 122 us -> none  [the longest x1 62.5 us: on_device(): square_total = lax.psum(jnp.sum(attended * attended, axis=1), 'tp')]
    pallas_call x0 -> x1, Pallas kernels: none -> 89.9 us  [on_device(): pl.pallas_call(functools.partial(kernel, chips), out_shape=(jax.ShapeDtyp...]
    dot_general x14 -> x0, matrix products: 23.4 us -> none  [the longest x1 3.75 us: on_device(): lax.dot_general(lax.all_gather(normed, 'tp', axis=1, tiled=True), weight_...]
    all_gather x1 -> x0, blocking collectives: 20.7 us -> none  [prefix(): lax.all_gather(a.astype(kind), axis)]
    add x15 -> x0, other arithmetic: 13.9 us -> none  [combine_states(): jnp.exp(later[0])[..., None, None] * earlier[1] + later[1]]
    exp x16 -> x0, other arithmetic: 9.7 us -> none  [the longest x15 9.63 us: combine_states(): jnp.exp(later[0])[..., None, None] * earlier[1] + later[1]]
  transfers between devices with their start and end apart: 4 -> 0, of which waited for: 4 -> 0; matrix products, arithmetic and copies ran while one was open for 1% -> 0% of each run, Pallas kernels for 0% -> 0%
where the time goes in v1:
time: 103 us; the launch traced here: 102 us
  Pallas kernels  89.9 us (87%)
  local copies, waits for them, and re-layouts  11.3 us (11%)
    pallas_call x1, Pallas kernels, on_device(): pl.pallas_call(functools.partial(kernel, chips), out_shape=(jax.ShapeDtyp...  89.9 us
    unnamed x18, local copies, waits for them, and re-layouts  10.6 us

profile of v1, /device:TPU:1, one launch (start us, length us, event | category | flops | bytes accessed | tf_op | source)
XLA Modules:
  0.0 101.9 jit_solution(7234808858577971562)
XLA Ops:
  0.6 0.8 copy.13.ld_ref
  1.4 1.0 copy.14.target_ref
  2.4 0.0 copy-start
  2.5 1.9 %copy-done = bf16[192,8192]{1,0:T(8,128)(2,1)S(1)} copy-done((bf16[192,8192]{1,0:T(8,128)(2,1)S(1)}, bf16[192,8192]{1,0:T(8,128)(2,1)}, u32[]{:S(2)}) %copy-start) | copy-done | bytes 3145752
  4.3 0.0 copy-start.1
  4.3 0.9 copy-done.1
  5.2 0.0 copy-start.2
  5.2 0.9 copy-done.2
  6.2 0.0 copy-start.3
  6.2 0.9 copy-done.3
  7.1 0.0 copy-start.4
  7.1 0.9 copy-done.4
  8.0 0.0 copy-start.5
  8.0 0.7 copy-done.5
  8.6 89.9 %attention_layer.1 = (bf16[256,192]{1,0:T(8,128)(2,1)S(1)}, bf16[256,256]{1,0:T(8,128)(2,1)S(1)}, bf16[256,256]{1,0:T(8,128)(2,1)S(1)}, bf16[256,256]{1,0:T(8,128)(2,1)S(1)}, bf16[256,256]{1,0:T(8,128)(2,1)S(1)}) custom-call(bf16[256,256]{1,0:T(8,128)(2,1)S(1)} %copy-done.1, bf16[256,256]{1,0:T(8,128)(2,1)S(1)} %copy-done.2, bf16[256,256]{1,0:T(8,128)(2,1)S(1)} %copy-done.3, ...), custom_call_target="tpu_custom_call" | custom-call | flops 2000000000 | bytes 8000000 | tf_op jit(solution)/shard_map/attention_layer/pallas_call | solution.py:629
  98.5 0.7 copy.15
  99.3 0.7 copy.20
  99.9 0.7 copy.21
  100.6 0.7 copy.22
  101.2 0.7 copy.23
Async XLA Ops:
  2.4 1.9 %copy-start = (bf16[192,8192]{1,0:T(8,128)(2,1)S(1)}, bf16[192,8192]{1,0:T(8,128)(2,1)}, u32[]{:S(2)}) copy-start(bf16[192,8192]{1,0:T(8,128)(2,1)} %w_ref.1) | copy-start | bytes 9437188
  4.3 0.9 copy-start.1
  5.2 0.9 copy-start.2
  6.2 0.9 copy-start.3
  7.1 0.9 copy-start.4
  8.0 0.7 copy-start.5

commit v2 on v1

--- a/solution.py
+++ b/solution.py
@@ -43,19 +43,27 @@
 
 def kernel(
     sizes,
+    q_in,
+    k_in,
+    v_in,
+    ld_in,
+    gate_in,
+    gain_in,
+    w_ref,
+    target_in,
+    out_ref,
+    qg_ref,
+    kg_ref,
+    vg_ref,
+    gg_ref,
     q_ref,
     k_ref,
     v_ref,
     ld_ref,
     gate_ref,
     gain_ref,
-    w_ref,
     target_ref,
-    out_ref,
-    qg_ref,
-    kg_ref,
-    vg_ref,
-    gg_ref,
+    in_sems,
     wb,
     wrelay,
     uall,
@@ -72,7 +80,6 @@
     att,
     klocal,
     vlocal,
-    targett,
     agrad,
     bown,
     bsib,
@@ -166,13 +173,28 @@
     def arrived(ref, sem):
         pltpu.make_async_copy(ref, ref, sem).wait()
 
+    loads = [
+        pltpu.make_async_copy(src, dst, in_sems.at[index])
+        for index, (src, dst) in enumerate(
+            (
+                (ld_in, ld_ref),
+                (k_in, k_ref),
+                (v_in, v_ref),
+                (q_in, q_ref),
+                (gate_in, gate_ref),
+                (gain_in, gain_ref),
+                (target_in, target_ref),
+            )
+        )
+    ]
+    for load in loads:
+        load.start()
     barrier = pltpu.get_barrier_semaphore()
     partners = [sibling] + [at_x(step) for step in range(1, X)]
     partners += [at_z(step) for step in range(1, Z)]
     partners += [at_y(lax.rem(y + step, Y)) for step in range(1, Y)]
     for partner in partners:
         pl.semaphore_signal(barrier, inc=1, device_id=partner, device_id_type=MESH)
-    pl.semaphore_wait(barrier, len(partners))
 
     def w_columns(block, x_to):
         start = pl.multiple_of((block * X + x_to) * width, width)
@@ -197,26 +219,25 @@
             ).start()
         return carry
 
-    lax.fori_loop(0, Z, w_far, 0)
-    lax.fori_loop(0, Z, w_near, 0)
-    lax.fori_loop(0, Z, w_mine, 0)
-
     row = lax.broadcasted_iota(jnp.int32, (tokens, tokens), 0)
     column = lax.broadcasted_iota(jnp.int32, (tokens, tokens), 1)
     causal = row >= column
+    loads[0].wait()
     cum = lax.dot_general(
-        jnp.where(causal, 1.0, 0.0).astype(F32),
         ld_ref[...],
+        jnp.where(row <= column, 1.0, 0.0).astype(F32),
         (((1,), (0,)), ((), ())),
         precision=lax.Precision.HIGHEST,
         preferred_element_type=F32,
     )
-    cums = [cum[:, h : h + 1] for h in range(heads)]
+    cum_rows = [cum[h : h + 1, :] for h in range(heads)]
+    cums = [as_columns(c) for c in cum_rows]
     totals = [c[tokens - 1 : tokens, :] for c in cums]
     bown[...] = jnp.zeros_like(bown)
     for h in range(heads):
-        bown[h : h + 1, :] = jnp.broadcast_to(totals[h], (1, 128))
-    send(bown, bsib, b_send, b_recv, sibling)
+        bown[h : h + 1, :] = totals[h]
+    loads[1].wait()
+    loads[2].wait()
 
     def lanes(h):
         return slice(h * DH, (h + 1) * DH)
@@ -292,7 +313,12 @@
         send(c_out.at[turn], state.at[turn, core], c_send.at[turn], c_recv.at[turn], sibling)
         arrived(c_out.at[turn], c_recv.at[turn])
 
+    pl.semaphore_wait(barrier, len(partners))
     scan_share(0, own)
+    send(bown, bsib, b_send, b_recv, sibling)
+    lax.fori_loop(0, Z, w_far, 0)
+    lax.fori_loop(0, Z, w_near, 0)
+    lax.fori_loop(0, Z, w_mine, 0)
 
     arrived(bsib, b_recv)
     bchip[y] = bown[...] + bsib[...]
@@ -301,13 +327,14 @@
         send(bchip.at[y], bchip.at[y], bc_send.at[distance - 1], bc_recv.at[distance - 1], at_y(place))
     scan_send(0)
 
+    for load in loads[3:]:
+        load.wait()
     for h in range(heads):
-        gaps = cums[h] - as_row(cums[h])
+        gaps = cums[h][:, 0:1] - cum_rows[h]
         decay = jnp.where(causal, jnp.exp(jnp.minimum(gaps, 0.0)), 0.0)
         weight[h] = decay
         probs[h] = (nt(q_ref[:, lanes(h)], k_ref[:, lanes(h)]) * decay).astype(BF16)
         att[:, lanes(h)] = nn(probs[h], v_ref[:, lanes(h)])
-    targett[...] = nt(identity(rows), target_ref[...])
 
     for distance in range(1, Y):
         arrived(bchip.at[lax.rem(y - distance + Y, Y)], bc_recv.at[distance - 1])
@@ -419,15 +446,14 @@
     inv_rms = lax.rsqrt(mean_square + EPS)
 
     product = jnp.zeros((1, tokens), F32)
-    outs = []
     for part in range(2):
         for kind in (1, 2):
             arrived(yrecv.at[kind, part], y_recv.at[kind, part])
         total = yacc[x, part] + yrecv[1, part].astype(F32) + yrecv[2, part].astype(F32)
         out_half = (total * inv_rms).astype(BF16)
-        grad = (out_half.astype(F32) - targett[part * half : (part + 1) * half, :]).astype(BF16)
+        grad = (out_half.astype(F32) - target_ref[part * half : (part + 1) * half, :].astype(F32)).astype(BF16)
         gx[x, part] = grad
-        outs.append(out_half)
+        out_ref[part * half : (part + 1) * half, :] = out_half
         product = product + jnp.sum(grad.astype(F32) * total, axis=0, keepdims=True)
 
     def g_start(source, part, kind, device):
@@ -440,7 +466,6 @@
     g_start(x, 0, 1, at_x(-1))
     small_share(1, product)
     eye = identity(tokens)
-    out_ref[...] = nt(eye, jnp.concatenate(outs, axis=0)).astype(BF16)
     arrived(gx.at[left, 0], g_recv.at[0, 0])
     g_start(left, 0, 2, at_x(1))
     arrived(gx.at[right, 1], g_recv.at[1, 1])
@@ -555,6 +580,16 @@
             arrived(small_x.at[turn, 0], sx_send.at[turn, distance - 1])
 
 
+def store(*refs):
+    count = len(refs) // 2
+    sems = refs[-1]
+    copies = [pltpu.make_async_copy(refs[i], refs[count + i], sems.at[i]) for i in range(count)]
+    for copy in copies:
+        copy.start()
+    for copy in copies:
+        copy.wait()
+
+
 def on_device(chips, queries, keys, values, log_decay, gate, norm_gain, out_weight, target):
     Y, Z = chips
     tokens, width = queries.shape
@@ -564,6 +599,14 @@
     vmem = pltpu.VMEM
     dma = pltpu.SemaphoreType.DMA
     scratch = [
+        vmem((tokens, width), BF16),
+        vmem((tokens, width), BF16),
+        vmem((tokens, width), BF16),
+        vmem((width // DH, tokens), F32),
+        vmem((tokens, width), BF16),
+        vmem((1, width), F32),
+        vmem((rows, tokens), BF16),
+        dma((7,)),
         vmem((Z, X, 2, half, width), BF16),
         vmem((Z, half, width), BF16),
         vmem((Z, tokens, width), BF16),
@@ -580,7 +623,6 @@
         vmem((tokens, width), F32),
         vmem((tokens, width), F32),
         vmem((tokens, width), F32),
-        vmem((rows, tokens), F32),
         vmem((tokens, width), BF16),
         vmem((8, 128), F32),
         vmem((8, 128), F32),
@@ -625,19 +667,31 @@
         dma((2, X - 1)),
     ]
     in_vmem = pl.BlockSpec(memory_space=pltpu.VMEM)
+    in_hbm = pl.BlockSpec(memory_space=pltpu.HBM)
     wide = jax.ShapeDtypeStruct((tokens, width), BF16)
-    return pl.pallas_call(
+    out_shape = (jax.ShapeDtypeStruct((rows, tokens), BF16), wide, wide, wide, wide)
+    results = pl.pallas_call(
         functools.partial(kernel, chips),
-        out_shape=(jax.ShapeDtypeStruct((tokens, rows), BF16), wide, wide, wide, wide),
-        in_specs=[in_vmem] * 6 + [pl.BlockSpec(memory_space=pl.ANY), in_vmem],
+        out_shape=out_shape,
+        in_specs=[in_hbm] * 8,
         out_specs=(in_vmem,) * 5,
         scratch_shapes=scratch,
         compiler_params=pltpu.CompilerParams(
-            collective_id=0, has_side_effects=True, vmem_limit_bytes=48 * 1024 * 1024
+            collective_id=0, has_side_effects=True, vmem_limit_bytes=63 * 1024 * 1024
         ),
         cost_estimate=pl.CostEstimate(flops=2 * 10**9, bytes_accessed=8 * 10**6, transcendentals=10**6),
         name="attention_layer",
-    )(queries, keys, values, log_decay, gate, norm_gain.reshape(1, width), out_weight, target)
+    )(queries, keys, values, log_decay.T, gate, norm_gain.reshape(1, width), out_weight, target.T)
+    output, *grads = pl.pallas_call(
+        store,
+        out_shape=out_shape,
+        in_specs=[pl.BlockSpec(memory_space=pl.ANY)] * 5,
+        out_specs=(in_hbm,) * 5,
+        scratch_shapes=[dma((5,))],
+        compiler_params=pltpu.CompilerParams(vmem_limit_bytes=63 * 1024 * 1024),
+        name="store",
+    )(*results)
+    return (output.T, *grads)
 
 
 def solution(mesh):

time: 103 us -> 113 us (1.097)
  Pallas kernels: 89.9 us -> 111 us
  local copies, waits for them, and re-layouts: 11.3 us -> 0 us
    pallas_call x1 -> x2, Pallas kernels: 89.9 us -> 111 us  [the longest x1 90.8 us: on_device(): pl.pallas_call(functools.partial(kernel, chips), out_shape=out_shape, in_...]
    unnamed x18 -> x0, local copies, waits for them, and re-layouts: 10.6 us -> none
where the time goes in v2:
time: 113 us; the launch traced here: 111 us
  Pallas kernels  111 us (98%)
    pallas_call x1, Pallas kernels, on_device(): pl.pallas_call(functools.partial(kernel, chips), out_shape=out_shape, in_...  90.8 us
    pallas_call x1, Pallas kernels, on_device(): pl.pallas_call(store, out_shape=out_shape, in_specs=[pl.BlockSpec(memory_...  20 us

profile of v2, /device:TPU:1, one launch (start us, length us, event | category | flops | bytes accessed | tf_op | source)
XLA Modules:
  0.0 111.5 jit_solution(869381575803336399)
XLA Ops:
  0.6 90.8 %attention_layer.1 = (bf16[192,256]{1,0:T(8,128)(2,1)}, bf16[256,256]{1,0:T(8,128)(2,1)}, bf16[256,256]{1,0:T(8,128)(2,1)}, bf16[256,256]{1,0:T(8,128)(2,1)}, bf16[256,256]{1,0:T(8,128)(2,1)}) custom-call(bf16[256,256]{1,0:T(8,128)(2,1)} %q_in.1, bf16[256,256]{1,0:T(8,128)(2,1)} %k_in.1, bf16[256,256]{1,0:T(8,128)(2,1)} %v_in.1, f32[2,256]{1,0:T(2,128)} %bitcast.6, ...), custom_call_target="tpu_custom_call" | custom-call | flops 2000000000 | bytes 8000000 | tf_op jit(solution)/shard_map/attention_layer/pallas_call | solution.py:673
  91.5 20.0 %store.1 = (bf16[192,256]{1,0:T(8,128)(2,1)}, bf16[256,256]{1,0:T(8,128)(2,1)}, bf16[256,256]{1,0:T(8,128)(2,1)}, bf16[256,256]{1,0:T(8,128)(2,1)}, bf16[256,256]{1,0:T(8,128)(2,1)}) custom-call(bf16[192,256]{1,0:T(8,128)(2,1)} %get-tuple-element.15.refs_0_, bf16[256,256]{1,0:T(8,128)(2,1)} %get-tuple-element.16.refs_1_, ...), custom_call_target="tpu_custom_call" | custom-call | tf_op jit(solution)/shard_map/store/pallas_call | solution.py:685

commit v3 on v2

--- a/solution.py
+++ b/solution.py
@@ -51,11 +51,17 @@
     gain_in,
     w_ref,
     target_in,
+    out_to,
+    qg_to,
+    kg_to,
+    vg_to,
+    gg_to,
     out_ref,
     qg_ref,
     kg_ref,
     vg_ref,
     gg_ref,
+    out_sems,
     q_ref,
     k_ref,
     v_ref,
@@ -219,6 +225,10 @@
             ).start()
         return carry
 
+    pl.semaphore_wait(barrier, len(partners))
+    lax.fori_loop(0, Z, w_far, 0)
+    lax.fori_loop(0, Z, w_near, 0)
+
     row = lax.broadcasted_iota(jnp.int32, (tokens, tokens), 0)
     column = lax.broadcasted_iota(jnp.int32, (tokens, tokens), 1)
     causal = row >= column
@@ -236,6 +246,7 @@
     bown[...] = jnp.zeros_like(bown)
     for h in range(heads):
         bown[h : h + 1, :] = totals[h]
+    send(bown, bsib, b_send, b_recv, sibling)
     loads[1].wait()
     loads[2].wait()
 
@@ -251,10 +262,15 @@
     def of_core(pair):
         return jnp.where(is_zero, pair[0], pair[1])
 
-    def scan_share(turn, states):
-        s_out[turn] = of_core((states[1], states[0])).astype(BF16)
-        s_keep[turn] = of_core((states[0], states[1]))
-        send(s_out.at[turn], s_in.at[turn], s_send.at[turn], s_recv.at[turn], sibling)
+    def scan_give(turn, h, value):
+        @pl.when(core == h)
+        def _():
+            s_keep[turn] = value
+
+        @pl.when(core != h)
+        def _():
+            s_out[turn] = value.astype(BF16)
+            send(s_out.at[turn], s_in.at[turn], s_send.at[turn], s_recv.at[turn], sibling)
 
     def scan_way(turn):
         step = 1 if turn == 0 else -1
@@ -313,11 +329,8 @@
         send(c_out.at[turn], state.at[turn, core], c_send.at[turn], c_recv.at[turn], sibling)
         arrived(c_out.at[turn], c_recv.at[turn])
 
-    pl.semaphore_wait(barrier, len(partners))
-    scan_share(0, own)
-    send(bown, bsib, b_send, b_recv, sibling)
-    lax.fori_loop(0, Z, w_far, 0)
-    lax.fori_loop(0, Z, w_near, 0)
+    for h in range(heads):
+        scan_give(0, h, own[h])
     lax.fori_loop(0, Z, w_mine, 0)
 
     arrived(bsib, b_recv)
@@ -352,14 +365,16 @@
         att[:, lanes(h)] = attended
         squares = squares + jnp.sum(attended * attended, axis=1, keepdims=True)
         gate_open = jax.nn.sigmoid(gate_ref[:, lanes(h)].astype(F32))
-        uall[z, :, lanes(h)] = (attended * gain[:, lanes(h)] * gate_open).astype(BF16)
+        gated = (attended * gain[:, lanes(h)] * gate_open).astype(BF16)
+        for part in range(2):
+            uall[z, part, :, lanes(h)] = gated[part * half_tokens : (part + 1) * half_tokens, :]
 
     far, near = Z // 2, Z - 1 - Z // 2
     hops = (far, near)
     ways = (sign, -sign)
 
     def u_part(way, step, part):
-        return uall.at[zs(-ways[way] * step), pl.ds(part * half_tokens, half_tokens)]
+        return uall.at[zs(-ways[way] * step), part]
 
     def u_start(way, step, part):
         ref = u_part(way, step, part)
@@ -402,134 +417,170 @@
 
     w_pair(left, w_recv.at[1], 0)
     w_pair(right, w_recv.at[2], 1)
+
+    def w_block(block):
+        return wb[block].reshape(X * rows, width)
+
+    def accumulate(block, part):
+        yacc[part] += nt(w_block(block), uall[block, part]).reshape(yacc.shape[1:])
+
+    def u_pass(step, part):
+        for way in range(2):
+            if step < hops[way]:
+                arrived(u_part(way, step + 1, part), u_recv.at[way, step, part])
+                if step + 1 < hops[way]:
+                    u_start(way, step + 1, part)
+
+    for step in range(far - 1):
+        for part in range(2):
+            u_pass(step, part)
+    small_cross(0)
     w_pair(opp, w_recv.at[3], 2)
     for part in range(2):
         arrived(wb.at[:, x, part], w_own)
     for slot, source in enumerate((left, right, opp)):
         arrived(wb.at[:, source, 1 - core], ws_recv.at[slot])
-
-    def w_block(block):
-        return wb[block].reshape(X * rows, width)
-
-    yacc[...] = nt(w_block(z), uall[z]).reshape(yacc.shape)
-
-    def accumulate(block):
-        yacc[...] += nt(w_block(block), uall[block]).reshape(yacc.shape)
+    for part in range(2):
+        yacc[part] = nt(w_block(z), uall[z, part]).reshape(yacc.shape[1:])
+        for step in range(far - 1):
+            for way in range(2):
+                if step < hops[way]:
+                    accumulate(zs(-ways[way] * (step + 1)), part)
+
+    def y_start(part, kind, piece, value, device):
+        ystage[part, kind, piece] = value.astype(BF16)
+        send(
+            ystage.at[part, kind, piece],
+            yrecv.at[part, kind, piece],
+            y_send.at[part, kind, piece],
+            y_recv.at[part, kind, piece],
+            device,
+        )
+
+    def y_arrived(part, kind, piece):
+        arrived(yrecv.at[part, kind, piece], y_recv.at[part, kind, piece])
+        return yrecv[part, kind, piece].astype(F32)
+
+    for part in range(2):
+        u_pass(far - 1, part)
+        for way in range(2):
+            if far == hops[way]:
+                accumulate(zs(-ways[way] * far), part)
+        y_start(part, 0, 0, yacc[part, opp, 0], at_x(1))
+        y_start(part, 0, 1, yacc[part, opp, 1], at_x(-1))
+        y_start(part, 1, 1, yacc[part, right, 1], at_x(1))
+        y_start(part, 1, 0, yacc[part, left, 0], at_x(-1))
+    for part in range(2):
+        y_start(part, 2, 0, yacc[part, right, 0] + y_arrived(part, 0, 0), at_x(1))
+        y_start(part, 2, 1, yacc[part, left, 1] + y_arrived(part, 0, 1), at_x(-1))
+
+    inv_rms = lax.rsqrt(small_sum(0) / total_features + EPS)
+
+    def g_start(part, source, piece, kind, device):
+        ref = gx.at[part, source, piece]
+        send(ref, ref, g_send.at[part, kind, piece], g_recv.at[part, kind, piece], device)
+
+    def g_arrived(part, source, piece, kind):
+        arrived(gx.at[part, source, piece], g_recv.at[part, kind, piece])
+
+    products = []
+    for part in range(2):
+        span = slice(part * half_tokens, (part + 1) * half_tokens)
+        product = jnp.zeros((1, half_tokens), F32)
+        for piece in range(2):
+            total = yacc[part, x, piece] + y_arrived(part, 1, piece) + y_arrived(part, 2, piece)
+            rounded = (total * inv_rms[:, span]).astype(BF16)
+            out_ref[piece * half : (piece + 1) * half, span] = rounded
+            wanted = target_ref[piece * half : (piece + 1) * half, span].astype(F32)
+            grad = (rounded.astype(F32) - wanted).astype(BF16)
+            gx[part, x, piece] = grad
+            g_start(part, x, piece, piece, at_x(1 - 2 * piece))
+            product = product + jnp.sum(grad.astype(F32) * total, axis=0, keepdims=True)
+        g_start(part, x, 1, 0, at_x(1))
+        g_start(part, x, 0, 1, at_x(-1))
+        products.append(product)
+    small_share(1, jnp.concatenate(products, axis=1))
+    stores = [
+        pltpu.make_async_copy(src, dst, out_sems.at[index])
+        for index, (src, dst) in enumerate(
+            ((out_ref, out_to), (qg_ref, qg_to), (kg_ref, kg_to), (vg_ref, vg_to), (gg_ref, gg_to))
+        )
+    ]
+    stores[0].start()
+    for part in range(2):
+        g_arrived(part, left, 0, 0)
+        g_start(part, left, 0, 2, at_x(1))
+        g_arrived(part, right, 1, 1)
+        g_start(part, right, 1, 2, at_x(-1))
+
+    eye = identity(half_tokens)
+
+    def feature_part(block, part):
+        return nn(gall[part], w_block(block))
+
+    def f_slot(way, step):
+        return way * far + step
+
+    def f_start(way, step, part, h, value):
+        slot = f_slot(way, step)
+        fstage[slot, part, h] = value.astype(BF16)
+        send(
+            fstage.at[slot, part, h],
+            frecv.at[slot, part, h],
+            f_send.at[slot, part, h],
+            f_recv.at[slot, part, h],
+            at_z(ways[way]),
+        )
+
+    def f_arrived(way, step, part, h):
+        slot = f_slot(way, step)
+        arrived(frecv.at[slot, part, h], f_recv.at[slot, part, h])
+        return frecv[slot, part, h].astype(F32)
 
     for step in range(far):
         for part in range(2):
+            if step == 0:
+                g_arrived(part, left, 1, 0)
+                g_arrived(part, right, 0, 1)
+                for piece in range(2):
+                    g_arrived(part, opp, piece, 2)
+                gall[part] = nt(eye, gx[part].reshape(X * rows, half_tokens)).astype(BF16)
+            sums = [
+                feature_part(zs(ways[way] * (hops[way] - step)), part) if step < hops[way] else None
+                for way in range(2)
+            ]
+            for h in range(heads):
+                for way in range(2):
+                    if step < hops[way]:
+                        value = sums[way][:, lanes(h)]
+                        if step > 0:
+                            value = value + f_arrived(way, step - 1, part, h)
+                        f_start(way, step, part, h, value)
+        if step == 0:
+            small_cross(1)
+
+    own_feature = [feature_part(z, part) for part in range(2)]
+    mean_product = as_columns(small_sum(1) / total_features)
+    inv = as_columns(inv_rms)
+
+    for h in range(heads):
+        pieces = []
+        for part in range(2):
+            value = own_feature[part][:, lanes(h)]
             for way in range(2):
-                if step < hops[way]:
-                    arrived(u_part(way, step + 1, part), u_recv.at[way, step, part])
-                    if step + 1 < hops[way]:
-                        u_start(way, step + 1, part)
-        for way in range(2):
-            if step < hops[way]:
-                accumulate(zs(-ways[way] * (step + 1)))
-
-    small_cross(0)
-
-    def y_start(kind, part, value, device):
-        ystage[kind, part] = value.astype(BF16)
-        send(ystage.at[kind, part], yrecv.at[kind, part], y_send.at[kind, part], y_recv.at[kind, part], device)
-
-    y_start(0, 0, yacc[opp, 0], at_x(1))
-    y_start(0, 1, yacc[opp, 1], at_x(-1))
-    y_start(1, 1, yacc[right, 1], at_x(1))
-    y_start(1, 0, yacc[left, 0], at_x(-1))
-    arrived(yrecv.at[0, 0], y_recv.at[0, 0])
-    y_start(2, 0, yacc[right, 0] + yrecv[0, 0].astype(F32), at_x(1))
-    arrived(yrecv.at[0, 1], y_recv.at[0, 1])
-    y_start(2, 1, yacc[left, 1] + yrecv[0, 1].astype(F32), at_x(-1))
-
-    mean_square = small_sum(0) / total_features
-    inv_rms = lax.rsqrt(mean_square + EPS)
-
-    product = jnp.zeros((1, tokens), F32)
-    for part in range(2):
-        for kind in (1, 2):
-            arrived(yrecv.at[kind, part], y_recv.at[kind, part])
-        total = yacc[x, part] + yrecv[1, part].astype(F32) + yrecv[2, part].astype(F32)
-        out_half = (total * inv_rms).astype(BF16)
-        grad = (out_half.astype(F32) - target_ref[part * half : (part + 1) * half, :].astype(F32)).astype(BF16)
-        gx[x, part] = grad
-        out_ref[part * half : (part + 1) * half, :] = out_half
-        product = product + jnp.sum(grad.astype(F32) * total, axis=0, keepdims=True)
-
-    def g_start(source, part, kind, device):
-        ref = gx.at[source, part]
-        send(ref, ref, g_send.at[kind, part], g_recv.at[kind, part], device)
-
-    g_start(x, 0, 0, at_x(1))
-    g_start(x, 1, 1, at_x(-1))
-    g_start(x, 1, 0, at_x(1))
-    g_start(x, 0, 1, at_x(-1))
-    small_share(1, product)
-    eye = identity(tokens)
-    arrived(gx.at[left, 0], g_recv.at[0, 0])
-    g_start(left, 0, 2, at_x(1))
-    arrived(gx.at[right, 1], g_recv.at[1, 1])
-    g_start(right, 1, 2, at_x(-1))
-    arrived(gx.at[left, 1], g_recv.at[0, 1])
-    arrived(gx.at[right, 0], g_recv.at[1, 0])
-    small_cross(1)
-    for part in range(2):
-        arrived(gx.at[opp, part], g_recv.at[2, part])
-    gall[...] = nt(eye, gx[...].reshape(X * rows, tokens)).astype(BF16)
-
-    def feature_part(block):
-        return nn(gall[...], w_block(block))
-
-    def f_slot(way, step):
-        return way * far + step
-
-    def f_start(way, step, part, value):
-        piece = pl.ds(part * half_tokens, half_tokens)
-        slot = f_slot(way, step)
-        fstage[slot, piece] = value.astype(BF16)
-        send(fstage.at[slot, piece], frecv.at[slot, piece], f_send.at[slot, part], f_recv.at[slot, part], at_z(ways[way]))
-
-    def f_arrived(way, step, part):
-        piece = pl.ds(part * half_tokens, half_tokens)
-        slot = f_slot(way, step)
-        arrived(frecv.at[slot, piece], f_recv.at[slot, part])
-        return frecv[slot, piece].astype(F32)
-
-    for step in range(far):
-        sums = [feature_part(zs(ways[way] * (hops[way] - step))) if step < hops[way] else None for way in range(2)]
-        for part in range(2):
-            for way in range(2):
-                if step < hops[way]:
-                    value = sums[way][part * half_tokens : (part + 1) * half_tokens, :]
-                    if step > 0:
-                        value = value + f_arrived(way, step - 1, part)
-                    f_start(way, step, part, value)
-
-    own_feature = feature_part(z)
-    mean_product = small_sum(1) / total_features
-    inv = as_columns(inv_rms)
-    mean_product = as_columns(mean_product)
-    feature = []
-    for part in range(2):
-        value = own_feature[part * half_tokens : (part + 1) * half_tokens, :]
-        for way in range(2):
-            if hops[way] > 0:
-                value = value + f_arrived(way, hops[way] - 1, part)
-        feature.append(value)
-    feature_grad = jnp.concatenate(feature, axis=0)
-
-    own = []
-    for h in range(heads):
+                if hops[way] > 0:
+                    value = value + f_arrived(way, hops[way] - 1, part, h)
+            pieces.append(value)
         attended = att[:, lanes(h)]
         gate_open = jax.nn.sigmoid(gate_ref[:, lanes(h)].astype(F32))
-        normed_grad = feature_grad[:, lanes(h)] * gain[:, lanes(h)] * gate_open
-        gg_ref[:, lanes(h)] = (normed_grad * attended * inv * (1.0 - gate_open)).astype(BF16)
+        normed_grad = jnp.concatenate(pieces, axis=0) * gain[:, lanes(h)] * gate_open
         grad = (inv * normed_grad - inv * inv * inv * attended * mean_product).astype(BF16)
         agrad[:, lanes(h)] = grad
         decayed = (q_ref[:, lanes(h)].astype(F32) * jnp.exp(cums[h])).astype(BF16)
-        own.append(tn(decayed, grad))
-
-    scan_share(1, own)
+        scan_give(1, h, tn(decayed, grad))
+        gg_ref[:, lanes(h)] = (normed_grad * attended * inv * (1.0 - gate_open)).astype(BF16)
+    stores[4].start()
+
     for h in range(heads):
         grad = agrad[:, lanes(h)]
         score_grad = (nt(grad, v_ref[:, lanes(h)]) * weight[h]).astype(BF16)
@@ -540,6 +591,7 @@
         ).astype(BF16)
         klocal[:, lanes(h)] = tn(score_grad, q_ref[:, lanes(h)])
         vlocal[:, lanes(h)] = tn(probs[h], grad)
+    stores[1].start()
     scan_end(1)
     for h in range(heads):
         later = state[1, h]
@@ -547,6 +599,9 @@
             klocal[:, lanes(h)] + jnp.exp(totals[h] - cums[h]) * nt(v_ref[:, lanes(h)], later)
         ).astype(BF16)
         vg_ref[:, lanes(h)] = (vlocal[:, lanes(h)] + nn(kdec[:, lanes(h)], later)).astype(BF16)
+
+    stores[2].start()
+    stores[3].start()
 
     for index in range(4):
         arrived(wrelay, w_send.at[index])
@@ -556,11 +611,14 @@
         for step in range(hops[way]):
             for part in range(2):
                 arrived(u_part(way, step, part), u_send.at[way, step, part])
-                arrived(u_part(way, step, part), f_send.at[f_slot(way, step), part])
-    for kind in range(3):
-        for part in range(2):
-            arrived(ystage.at[kind, part], y_send.at[kind, part])
-            arrived(ystage.at[kind, part], g_send.at[kind, part])
+                slot = f_slot(way, step)
+                for h in range(heads):
+                    arrived(fstage.at[slot, part, h], f_send.at[slot, part, h])
+    for part in range(2):
+        for kind in range(3):
+            for piece in range(2):
+                arrived(ystage.at[part, kind, piece], y_send.at[part, kind, piece])
+                arrived(ystage.at[part, kind, piece], g_send.at[part, kind, piece])
     arrived(bown, b_send)
     for distance in range(1, Y):
         arrived(bown, bc_send.at[distance - 1])
@@ -578,16 +636,14 @@
             arrived(small_z.at[turn, 0], sz_send.at[turn, distance - 1])
         for distance in range(1, X):
             arrived(small_x.at[turn, 0], sx_send.at[turn, distance - 1])
+    for copy in stores:
+        copy.wait()
 
 
 def store(*refs):
     count = len(refs) // 2
-    sems = refs[-1]
-    copies = [pltpu.make_async_copy(refs[i], refs[count + i], sems.at[i]) for i in range(count)]
-    for copy in copies:
-        copy.start()
-    for copy in copies:
-        copy.wait()
+    for src, dst in zip(refs[:count], refs[count:]):
+        dst[...] = src[...]
 
 
 def on_device(chips, queries, keys, values, log_decay, gate, norm_gain, out_weight, target):
@@ -599,6 +655,12 @@
     vmem = pltpu.VMEM
     dma = pltpu.SemaphoreType.DMA
     scratch = [
+        vmem((rows, tokens), BF16),
+        vmem((tokens, width), BF16),
+        vmem((tokens, width), BF16),
+        vmem((tokens, width), BF16),
+        vmem((tokens, width), BF16),
+        dma((5,)),
         vmem((tokens, width), BF16),
         vmem((tokens, width), BF16),
         vmem((tokens, width), BF16),
@@ -609,14 +671,14 @@
         dma((7,)),
         vmem((Z, X, 2, half, width), BF16),
         vmem((Z, half, width), BF16),
-        vmem((Z, tokens, width), BF16),
-        vmem((X, 2, half, tokens), F32),
-        vmem((3, 2, half, tokens), BF16),
-        vmem((3, 2, half, tokens), BF16),
-        vmem((X, 2, half, tokens), BF16),
-        vmem((tokens, X * rows), BF16),
-        vmem((Z - 1, tokens, width), BF16),
-        vmem((Z - 1, tokens, width), BF16),
+        vmem((Z, 2, tokens // 2, width), BF16),
+        vmem((2, X, 2, half, tokens // 2), F32),
+        vmem((2, 3, 2, half, tokens // 2), BF16),
+        vmem((2, 3, 2, half, tokens // 2), BF16),
+        vmem((2, X, 2, half, tokens // 2), BF16),
+        vmem((2, tokens // 2, X * rows), BF16),
+        vmem((Z - 1, 2, 2, tokens // 2, DH), BF16),
+        vmem((Z - 1, 2, 2, tokens // 2, DH), BF16),
         vmem((width // DH, tokens, tokens), F32),
         vmem((width // DH, tokens, tokens), BF16),
         vmem((tokens, width), BF16),
@@ -645,12 +707,12 @@
         dma((3,)),
         dma((2, far, 2)),
         dma((2, far, 2)),
-        dma((3, 2)),
-        dma((3, 2)),
-        dma((3, 2)),
-        dma((3, 2)),
-        dma((Z - 1, 2)),
-        dma((Z - 1, 2)),
+        dma((2, 3, 2)),
+        dma((2, 3, 2)),
+        dma((2, 3, 2)),
+        dma((2, 3, 2)),
+        dma((Z - 1, 2, 2)),
+        dma((Z - 1, 2, 2)),
         dma,
         dma,
         dma((max(Y - 1, 1),)),
@@ -674,7 +736,7 @@
         functools.partial(kernel, chips),
         out_shape=out_shape,
         in_specs=[in_hbm] * 8,
-        out_specs=(in_vmem,) * 5,
+        out_specs=(in_hbm,) * 5,
         scratch_shapes=scratch,
         compiler_params=pltpu.CompilerParams(
             collective_id=0, has_side_effects=True, vmem_limit_bytes=63 * 1024 * 1024
@@ -685,9 +747,8 @@
     output, *grads = pl.pallas_call(
         store,
         out_shape=out_shape,
-        in_specs=[pl.BlockSpec(memory_space=pl.ANY)] * 5,
-        out_specs=(in_hbm,) * 5,
-        scratch_shapes=[dma((5,))],
+        in_specs=[in_vmem] * 5,
+        out_specs=(in_vmem,) * 5,
         compiler_params=pltpu.CompilerParams(vmem_limit_bytes=63 * 1024 * 1024),
         name="store",
     )(*results)

time: 113 us -> 86.8 us (0.77); the launches traced: 111 us -> 86.7 us
  Pallas kernels: 111 us -> 86 us
    pallas_call x1, Pallas kernels: 20 us -> 1.97 us  [on_device(): pl.pallas_call(store, out_shape=out_shape, in_specs=[in_vmem] * 5, out_sp...]
    pallas_call x1, Pallas kernels: 90.8 us -> 84.1 us  [on_device(): pl.pallas_call(functools.partial(kernel, chips), out_shape=out_shape, in_...]
where the time goes in v3:
time: 86.8 us; the launch traced here: 86.7 us
  Pallas kernels  86 us (99%)
    pallas_call x1, Pallas kernels, on_device(): pl.pallas_call(functools.partial(kernel, chips), out_shape=out_shape, in_...  84.1 us
    pallas_call x1, Pallas kernels, on_device(): pl.pallas_call(store, out_shape=out_shape, in_specs=[in_vmem] * 5, out_sp...  1.97 us

profile of v3, /device:TPU:1, one launch (start us, length us, event | category | flops | bytes accessed | tf_op | source)
XLA Modules:
  0.0 86.7 jit_solution(5529104704829111301)
XLA Ops:
  0.6 84.1 %attention_layer.1 = (bf16[192,256]{1,0:T(8,128)(2,1)}, bf16[256,256]{1,0:T(8,128)(2,1)}, bf16[256,256]{1,0:T(8,128)(2,1)}, bf16[256,256]{1,0:T(8,128)(2,1)}, bf16[256,256]{1,0:T(8,128)(2,1)}) custom-call(bf16[256,256]{1,0:T(8,128)(2,1)} %q_in.1, bf16[256,256]{1,0:T(8,128)(2,1)} %k_in.1, bf16[256,256]{1,0:T(8,128)(2,1)} %v_in.1, f32[2,256]{1,0:T(2,128)} %bitcast.6, ...), custom_call_target="tpu_custom_call" | custom-call | flops 2000000000 | bytes 8000000 | tf_op jit(solution)/shard_map/attention_layer/pallas_call | solution.py:735
  84.7 2.0 %store.1 = (bf16[192,256]{1,0:T(8,128)(2,1)}, bf16[256,256]{1,0:T(8,128)(2,1)}, bf16[256,256]{1,0:T(8,128)(2,1)}, bf16[256,256]{1,0:T(8,128)(2,1)}, bf16[256,256]{1,0:T(8,128)(2,1)}) custom-call(bf16[192,256]{1,0:T(8,128)(2,1)} %get-tuple-element.15.refs_0_, bf16[256,256]{1,0:T(8,128)(2,1)} %get-tuple-element.16.refs_1_, ...), custom_call_target="tpu_custom_call" | custom-call | tf_op jit(solution)/shard_map/store/pallas_call | solution.py:747

commit v4 on v3

--- a/solution.py
+++ b/solution.py
@@ -106,6 +106,8 @@
     w_own,
     ws_send,
     ws_recv,
+    wy_send,
+    wy_recv,
     u_send,
     u_recv,
     y_send,
@@ -209,25 +211,33 @@
     my_rows = pl.ds(pl.multiple_of(core * half, half), half)
     x_far = xs(sign)
 
-    def w_far(block, carry):
-        send(w_ref.at[my_rows, w_columns(block, opp)], wrelay.at[block], w_send.at[0], w_recv.at[0], (ctx, z * X + x_far))
+    odd = lax.rem(y, 2)
+
+    def w_far(place, carry):
+        columns = w_columns(2 * place + odd, opp)
+        send(w_ref.at[my_rows, columns], wrelay.at[place], w_send.at[0], w_recv.at[0], (ctx, z * X + x_far))
         return carry
 
-    def w_near(block, carry):
-        send(w_ref.at[my_rows, w_columns(block, right)], wb.at[block, x, core], w_send.at[1], w_recv.at[1], at_x(1))
-        send(w_ref.at[my_rows, w_columns(block, left)], wb.at[block, x, core], w_send.at[2], w_recv.at[2], at_x(-1))
+    def w_near(place, carry):
+        block = 2 * place + odd
+        slot = wb.at[odd, place, x, core]
+        send(w_ref.at[my_rows, w_columns(block, right)], slot, w_send.at[1], w_recv.at[1], at_x(1))
+        send(w_ref.at[my_rows, w_columns(block, left)], slot, w_send.at[2], w_recv.at[2], at_x(-1))
         return carry
 
-    def w_mine(block, carry):
-        for part in range(2):
-            pltpu.make_async_copy(
-                w_ref.at[pl.ds(part * half, half), w_columns(block, x)], wb.at[block, x, part], w_own
-            ).start()
+    def w_mine(place, carry):
+        for other in range(2):
+            for part in range(2):
+                pltpu.make_async_copy(
+                    w_ref.at[pl.ds(part * half, half), w_columns(2 * place + other, x)],
+                    wb.at[other, place, x, part],
+                    w_own,
+                ).start()
         return carry
 
     pl.semaphore_wait(barrier, len(partners))
-    lax.fori_loop(0, Z, w_far, 0)
-    lax.fori_loop(0, Z, w_near, 0)
+    lax.fori_loop(0, Z // 2, w_far, 0)
+    lax.fori_loop(0, Z // 2, w_near, 0)
 
     row = lax.broadcasted_iota(jnp.int32, (tokens, tokens), 0)
     column = lax.broadcasted_iota(jnp.int32, (tokens, tokens), 1)
@@ -331,7 +341,7 @@
 
     for h in range(heads):
         scan_give(0, h, own[h])
-    lax.fori_loop(0, Z, w_mine, 0)
+    lax.fori_loop(0, Z // 2, w_mine, 0)
 
     arrived(bsib, b_recv)
     bchip[y] = bown[...] + bsib[...]
@@ -353,7 +363,7 @@
         arrived(bchip.at[lax.rem(y - distance + Y, Y)], bc_recv.at[distance - 1])
 
     arrived(wrelay, w_recv.at[0])
-    send(wrelay, wb.at[:, xs(-sign), core], w_send.at[3], w_recv.at[3], (ctx, z * X + x_far))
+    send(wrelay, wb.at[odd, :, xs(-sign), core], w_send.at[3], w_recv.at[3], (ctx, z * X + x_far))
 
     scan_end(0)
 
@@ -410,16 +420,26 @@
 
     small_share(0, as_row(squares))
 
-    def w_pair(source, sem, slot):
-        ref = wb.at[:, source, core]
-        arrived(ref, sem)
+    quarter = Z // 4
+
+    def w_span(parity, source, way):
+        return wb.at[parity, pl.ds(way * quarter, quarter), source, core]
+
+    def w_pair(parity, source, slot):
+        ref = wb.at[parity, :, source, core]
         send(ref, ref, ws_send.at[slot], ws_recv.at[slot], sibling)
 
-    w_pair(left, w_recv.at[1], 0)
-    w_pair(right, w_recv.at[2], 1)
+    for slot, source in enumerate((left, right, opp)):
+        arrived(wb.at[odd, :, source, core], w_recv.at[slot + 1])
+        for way in range(2):
+            ref = w_span(odd, source, way)
+            place = lax.rem(y + 1 - 2 * way + Y, Y)
+            send(ref, ref, wy_send.at[slot, way], wy_recv.at[slot, way], at_y(place))
+    for slot, source in enumerate((left, right, opp)):
+        w_pair(odd, source, slot)
 
     def w_block(block):
-        return wb[block].reshape(X * rows, width)
+        return wb[lax.rem(block, 2), lax.div(block, 2)].reshape(X * rows, width)
 
     def accumulate(block, part):
         yacc[part] += nt(w_block(block), uall[block, part]).reshape(yacc.shape[1:])
@@ -435,11 +455,14 @@
         for part in range(2):
             u_pass(step, part)
     small_cross(0)
-    w_pair(opp, w_recv.at[3], 2)
-    for part in range(2):
-        arrived(wb.at[:, x, part], w_own)
     for slot, source in enumerate((left, right, opp)):
-        arrived(wb.at[:, source, 1 - core], ws_recv.at[slot])
+        for way in range(2):
+            arrived(w_span(1 - odd, source, way), wy_recv.at[slot, way])
+        w_pair(1 - odd, source, 3 + slot)
+    arrived(wb.at[:, :, x], w_own)
+    for slot, source in enumerate((left, right, opp)):
+        arrived(wb.at[odd, :, source, 1 - core], ws_recv.at[slot])
+        arrived(wb.at[1 - odd, :, source, 1 - core], ws_recv.at[3 + slot])
     for part in range(2):
         yacc[part] = nt(w_block(z), uall[z, part]).reshape(yacc.shape[1:])
         for step in range(far - 1):
@@ -605,8 +628,11 @@
 
     for index in range(4):
         arrived(wrelay, w_send.at[index])
-    for index in range(3):
+    for index in range(6):
         arrived(wrelay, ws_send.at[index])
+    for slot in range(3):
+        for way in range(2):
+            arrived(w_span(odd, x, way), wy_send.at[slot, way])
     for way in range(2):
         for step in range(hops[way]):
             for part in range(2):
@@ -669,8 +695,8 @@
         vmem((1, width), F32),
         vmem((rows, tokens), BF16),
         dma((7,)),
-        vmem((Z, X, 2, half, width), BF16),
-        vmem((Z, half, width), BF16),
+        vmem((2, Z // 2, X, 2, half, width), BF16),
+        vmem((Z // 2, half, width), BF16),
         vmem((Z, 2, tokens // 2, width), BF16),
         vmem((2, X, 2, half, tokens // 2), F32),
         vmem((2, 3, 2, half, tokens // 2), BF16),
@@ -703,8 +729,10 @@
         dma((4,)),
         dma((4,)),
         dma,
-        dma((3,)),
-        dma((3,)),
+        dma((6,)),
+        dma((6,)),
+        dma((3, 2)),
+        dma((3, 2)),
         dma((2, far, 2)),
         dma((2, far, 2)),
         dma((2, 3, 2)),

time: 86.8 us -> 86.8 us (level)
  no operation moved by 1% of the time
where the time goes in v4:
time: 86.8 us; the launch traced here: 86.7 us
  Pallas kernels  86.1 us (99%)
    pallas_call x1, Pallas kernels, on_device(): pl.pallas_call(functools.partial(kernel, chips), out_shape=out_shape, in_...  84.1 us
    pallas_call x1, Pallas kernels, on_device(): pl.pallas_call(store, out_shape=out_shape, in_specs=[in_vmem] * 5, out_sp...  1.97 us

profile of v4, /device:TPU:1, one launch (start us, length us, event | category | flops | bytes accessed | tf_op | source)
XLA Modules:
  0.0 86.7 jit_solution(9461016414823565288)
XLA Ops:
  0.6 84.1 %attention_layer.1 = (bf16[192,256]{1,0:T(8,128)(2,1)}, bf16[256,256]{1,0:T(8,128)(2,1)}, bf16[256,256]{1,0:T(8,128)(2,1)}, bf16[256,256]{1,0:T(8,128)(2,1)}, bf16[256,256]{1,0:T(8,128)(2,1)}) custom-call(bf16[256,256]{1,0:T(8,128)(2,1)} %q_in.1, bf16[256,256]{1,0:T(8,128)(2,1)} %k_in.1, bf16[256,256]{1,0:T(8,128)(2,1)} %v_in.1, f32[2,256]{1,0:T(2,128)} %bitcast.6, ...), custom_call_target="tpu_custom_call" | custom-call | flops 2000000000 | bytes 8000000 | tf_op jit(solution)/shard_map/attention_layer/pallas_call | solution.py:763
  84.7 2.0 %store.1 = (bf16[192,256]{1,0:T(8,128)(2,1)}, bf16[256,256]{1,0:T(8,128)(2,1)}, bf16[256,256]{1,0:T(8,128)(2,1)}, bf16[256,256]{1,0:T(8,128)(2,1)}, bf16[256,256]{1,0:T(8,128)(2,1)}) custom-call(bf16[192,256]{1,0:T(8,128)(2,1)} %get-tuple-element.15.refs_0_, bf16[256,256]{1,0:T(8,128)(2,1)} %get-tuple-element.16.refs_1_, ...), custom_call_target="tpu_custom_call" | custom-call | tf_op jit(solution)/shard_map/store/pallas_call | solution.py:775

commit v5 on v3

--- a/solution.py
+++ b/solution.py
@@ -51,17 +51,11 @@
     gain_in,
     w_ref,
     target_in,
-    out_to,
-    qg_to,
-    kg_to,
-    vg_to,
-    gg_to,
     out_ref,
     qg_ref,
     kg_ref,
     vg_ref,
     gg_ref,
-    out_sems,
     q_ref,
     k_ref,
     v_ref,
@@ -87,6 +81,11 @@
     klocal,
     vlocal,
     agrad,
+    until_end,
+    from_start,
+    qdec,
+    scale,
+    closed,
     bown,
     bsib,
     bchip,
@@ -225,28 +224,23 @@
             ).start()
         return carry
 
-    pl.semaphore_wait(barrier, len(partners))
-    lax.fori_loop(0, Z, w_far, 0)
-    lax.fori_loop(0, Z, w_near, 0)
-
     row = lax.broadcasted_iota(jnp.int32, (tokens, tokens), 0)
     column = lax.broadcasted_iota(jnp.int32, (tokens, tokens), 1)
     causal = row >= column
     loads[0].wait()
-    cum = lax.dot_general(
-        ld_ref[...],
-        jnp.where(row <= column, 1.0, 0.0).astype(F32),
-        (((1,), (0,)), ((), ())),
-        precision=lax.Precision.HIGHEST,
-        preferred_element_type=F32,
-    )
+    upto = jnp.where(row <= column, 1.0, 0.0).astype(BF16)
+    rest = ld_ref[...]
+    cum = jnp.zeros_like(rest)
+    for _ in range(3):
+        piece = rest.astype(BF16)
+        cum = cum + nn(piece, upto)
+        rest = rest - piece.astype(F32)
     cum_rows = [cum[h : h + 1, :] for h in range(heads)]
     cums = [as_columns(c) for c in cum_rows]
     totals = [c[tokens - 1 : tokens, :] for c in cums]
     bown[...] = jnp.zeros_like(bown)
     for h in range(heads):
         bown[h : h + 1, :] = totals[h]
-    send(bown, bsib, b_send, b_recv, sibling)
     loads[1].wait()
     loads[2].wait()
 
@@ -255,7 +249,8 @@
 
     own = []
     for h in range(heads):
-        decayed = (k_ref[:, lanes(h)].astype(F32) * jnp.exp(totals[h] - cums[h])).astype(BF16)
+        until_end[h] = jnp.exp(totals[h] - cums[h])
+        decayed = (k_ref[:, lanes(h)].astype(F32) * until_end[h]).astype(BF16)
         kdec[:, lanes(h)] = decayed
         own.append(tn(decayed, v_ref[:, lanes(h)]))
 
@@ -327,10 +322,16 @@
         state[turn, core] = jnp.where(first_here, carried, after).astype(BF16)
         c_out[turn] = jnp.where(first_here, after, carried).astype(BF16)
         send(c_out.at[turn], state.at[turn, core], c_send.at[turn], c_recv.at[turn], sibling)
-        arrived(c_out.at[turn], c_recv.at[turn])
-
+
+    def scan_take(turn):
+        arrived(state.at[turn, 1 - core], c_recv.at[turn])
+
+    pl.semaphore_wait(barrier, len(partners))
+    send(bown, bsib, b_send, b_recv, sibling)
     for h in range(heads):
         scan_give(0, h, own[h])
+    lax.fori_loop(0, Z, w_far, 0)
+    lax.fori_loop(0, Z, w_near, 0)
     lax.fori_loop(0, Z, w_mine, 0)
 
     arrived(bsib, b_recv)
@@ -348,6 +349,11 @@
         weight[h] = decay
         probs[h] = (nt(q_ref[:, lanes(h)], k_ref[:, lanes(h)]) * decay).astype(BF16)
         att[:, lanes(h)] = nn(probs[h], v_ref[:, lanes(h)])
+        from_start[h] = jnp.exp(cums[h])
+        qdec[:, lanes(h)] = (q_ref[:, lanes(h)].astype(F32) * from_start[h]).astype(BF16)
+        gate_open = jax.nn.sigmoid(gate_ref[:, lanes(h)].astype(F32))
+        scale[:, lanes(h)] = gain_ref[:, lanes(h)] * gate_open
+        closed[:, lanes(h)] = 1.0 - gate_open
 
     for distance in range(1, Y):
         arrived(bchip.at[lax.rem(y - distance + Y, Y)], bc_recv.at[distance - 1])
@@ -356,18 +362,7 @@
     send(wrelay, wb.at[:, xs(-sign), core], w_send.at[3], w_recv.at[3], (ctx, z * X + x_far))
 
     scan_end(0)
-
-    gain = gain_ref[...]
-    squares = jnp.zeros((tokens, 1), F32)
-    for h in range(heads):
-        from_state = nn(q_ref[:, lanes(h)], state[0, h]) * jnp.exp(cums[h])
-        attended = att[:, lanes(h)] + from_state
-        att[:, lanes(h)] = attended
-        squares = squares + jnp.sum(attended * attended, axis=1, keepdims=True)
-        gate_open = jax.nn.sigmoid(gate_ref[:, lanes(h)].astype(F32))
-        gated = (attended * gain[:, lanes(h)] * gate_open).astype(BF16)
-        for part in range(2):
-            uall[z, part, :, lanes(h)] = gated[part * half_tokens : (part + 1) * half_tokens, :]
+    scan_take(0)
 
     far, near = Z // 2, Z - 1 - Z // 2
     hops = (far, near)
@@ -381,6 +376,12 @@
         send(ref, ref, u_send.at[way, step, part], u_recv.at[way, step, part], at_z(ways[way]))
 
     for part in range(2):
+        span = slice(part * half_tokens, (part + 1) * half_tokens)
+        for h in range(heads):
+            from_state = nn(q_ref[span, lanes(h)], state[0, h]) * from_start[h, span, :]
+            attended = att[span, lanes(h)] + from_state
+            att[span, lanes(h)] = attended
+            uall[z, part, :, lanes(h)] = (attended * scale[span, lanes(h)]).astype(BF16)
         for way in range(2):
             if hops[way] > 0:
                 u_start(way, 0, part)
@@ -408,15 +409,16 @@
             sum_x = sum_x + small_x[turn, step]
         return sum_x
 
+    squares = jnp.zeros((tokens, 1), F32)
+    for h in range(heads):
+        attended = att[:, lanes(h)]
+        squares = squares + jnp.sum(attended * attended, axis=1, keepdims=True)
     small_share(0, as_row(squares))
 
     def w_pair(source, sem, slot):
         ref = wb.at[:, source, core]
         arrived(ref, sem)
         send(ref, ref, ws_send.at[slot], ws_recv.at[slot], sibling)
-
-    w_pair(left, w_recv.at[1], 0)
-    w_pair(right, w_recv.at[2], 1)
 
     def w_block(block):
         return wb[block].reshape(X * rows, width)
@@ -431,21 +433,45 @@
                 if step + 1 < hops[way]:
                     u_start(way, step + 1, part)
 
+    def absorb(step):
+        for way in range(2):
+            if step < hops[way]:
+                for part in range(2):
+                    accumulate(zs(-ways[way] * (step + 1)), part)
+
+    def w_first():
+        w_pair(left, w_recv.at[1], 0)
+        w_pair(right, w_recv.at[2], 1)
+
+    def w_second():
+        small_cross(0)
+        w_pair(opp, w_recv.at[3], 2)
+
+    def w_third():
+        for part in range(2):
+            arrived(wb.at[:, x, part], w_own)
+        for slot, source in enumerate((left, right, opp)):
+            arrived(wb.at[:, source, 1 - core], ws_recv.at[slot])
+        for part in range(2):
+            yacc[part] = nt(w_block(z), uall[z, part]).reshape(yacc.shape[1:])
+
+    stages = [w_first, w_second, w_third]
+    ready = 0
     for step in range(far - 1):
         for part in range(2):
             u_pass(step, part)
-    small_cross(0)
-    w_pair(opp, w_recv.at[3], 2)
-    for part in range(2):
-        arrived(wb.at[:, x, part], w_own)
-    for slot, source in enumerate((left, right, opp)):
-        arrived(wb.at[:, source, 1 - core], ws_recv.at[slot])
-    for part in range(2):
-        yacc[part] = nt(w_block(z), uall[z, part]).reshape(yacc.shape[1:])
-        for step in range(far - 1):
-            for way in range(2):
-                if step < hops[way]:
-                    accumulate(zs(-ways[way] * (step + 1)), part)
+        if step < len(stages) - 1:
+            stages[step]()
+        if step == len(stages) - 2 or step == far - 2:
+            for stage in stages[min(step, len(stages) - 2) + 1 :]:
+                stage()
+            stages = []
+        if not stages:
+            while ready <= step:
+                absorb(ready)
+                ready += 1
+    for stage in stages:
+        stage()
 
     def y_start(part, kind, piece, value, device):
         ystage[part, kind, piece] = value.astype(BF16)
@@ -463,13 +489,21 @@
 
     for part in range(2):
         u_pass(far - 1, part)
-        for way in range(2):
-            if far == hops[way]:
-                accumulate(zs(-ways[way] * far), part)
+        last = zs(sign * far)
+        last_u = uall[last, part]
+
+        def finish(rows_of):
+            block = wb[last, rows_of].reshape(rows, width)
+            yacc[part, rows_of] += nt(block, last_u).reshape(yacc.shape[2:])
+
+        finish(opp)
         y_start(part, 0, 0, yacc[part, opp, 0], at_x(1))
         y_start(part, 0, 1, yacc[part, opp, 1], at_x(-1))
+        finish(right)
         y_start(part, 1, 1, yacc[part, right, 1], at_x(1))
+        finish(left)
         y_start(part, 1, 0, yacc[part, left, 0], at_x(-1))
+        finish(x)
     for part in range(2):
         y_start(part, 2, 0, yacc[part, right, 0] + y_arrived(part, 0, 0), at_x(1))
         y_start(part, 2, 1, yacc[part, left, 1] + y_arrived(part, 0, 1), at_x(-1))
@@ -500,13 +534,6 @@
         g_start(part, x, 0, 1, at_x(-1))
         products.append(product)
     small_share(1, jnp.concatenate(products, axis=1))
-    stores = [
-        pltpu.make_async_copy(src, dst, out_sems.at[index])
-        for index, (src, dst) in enumerate(
-            ((out_ref, out_to), (qg_ref, qg_to), (kg_ref, kg_to), (vg_ref, vg_to), (gg_ref, gg_to))
-        )
-    ]
-    stores[0].start()
     for part in range(2):
         g_arrived(part, left, 0, 0)
         g_start(part, left, 0, 2, at_x(1))
@@ -572,14 +599,11 @@
                     value = value + f_arrived(way, hops[way] - 1, part, h)
             pieces.append(value)
         attended = att[:, lanes(h)]
-        gate_open = jax.nn.sigmoid(gate_ref[:, lanes(h)].astype(F32))
-        normed_grad = jnp.concatenate(pieces, axis=0) * gain[:, lanes(h)] * gate_open
+        normed_grad = jnp.concatenate(pieces, axis=0) * scale[:, lanes(h)]
         grad = (inv * normed_grad - inv * inv * inv * attended * mean_product).astype(BF16)
         agrad[:, lanes(h)] = grad
-        decayed = (q_ref[:, lanes(h)].astype(F32) * jnp.exp(cums[h])).astype(BF16)
-        scan_give(1, h, tn(decayed, grad))
-        gg_ref[:, lanes(h)] = (normed_grad * attended * inv * (1.0 - gate_open)).astype(BF16)
-    stores[4].start()
+        scan_give(1, h, tn(qdec[:, lanes(h)], grad))
+        gg_ref[:, lanes(h)] = (normed_grad * attended * inv * closed[:, lanes(h)]).astype(BF16)
 
     for h in range(heads):
         grad = agrad[:, lanes(h)]
@@ -587,22 +611,10 @@
         if h == 0:
             scan_send(1)
         qg_ref[:, lanes(h)] = (
-            nn(score_grad, k_ref[:, lanes(h)]) + jnp.exp(cums[h]) * nt(grad, state[0, h])
+            nn(score_grad, k_ref[:, lanes(h)]) + from_start[h] * nt(grad, state[0, h])
         ).astype(BF16)
         klocal[:, lanes(h)] = tn(score_grad, q_ref[:, lanes(h)])
         vlocal[:, lanes(h)] = tn(probs[h], grad)
-    stores[1].start()
-    scan_end(1)
-    for h in range(heads):
-        later = state[1, h]
-        kg_ref[:, lanes(h)] = (
-            klocal[:, lanes(h)] + jnp.exp(totals[h] - cums[h]) * nt(v_ref[:, lanes(h)], later)
-        ).astype(BF16)
-        vg_ref[:, lanes(h)] = (vlocal[:, lanes(h)] + nn(kdec[:, lanes(h)], later)).astype(BF16)
-
-    stores[2].start()
-    stores[3].start()
-
     for index in range(4):
         arrived(wrelay, w_send.at[index])
     for index in range(3):
@@ -624,26 +636,42 @@
         arrived(bown, bc_send.at[distance - 1])
     for turn in range(2):
         arrived(s_out.at[turn], s_send.at[turn])
-        arrived(c_out.at[turn], c_send.at[turn])
-        step, _ = scan_way(turn)
-        for distance in range(1, Y):
-
-            @pl.when(reaches(y + step * distance))
-            def _():
-                arrived(t_out.at[turn], t_send.at[turn, distance - 1])
-
         for distance in range(1, Z):
             arrived(small_z.at[turn, 0], sz_send.at[turn, distance - 1])
         for distance in range(1, X):
             arrived(small_x.at[turn, 0], sx_send.at[turn, distance - 1])
-    for copy in stores:
+
+    def scan_sent(turn):
+        arrived(c_out.at[turn], c_send.at[turn])
+        step, _ = scan_way(turn)
+        for distance in range(1, Y):
+
+            @pl.when(reaches(y + step * distance))
+            def _():
+                arrived(t_out.at[turn], t_send.at[turn, distance - 1])
+
+    scan_sent(0)
+
+    scan_end(1)
+    scan_take(1)
+    for h in range(heads):
+        later = state[1, h]
+        kg_ref[:, lanes(h)] = (
+            klocal[:, lanes(h)] + until_end[h] * nt(v_ref[:, lanes(h)], later)
+        ).astype(BF16)
+        vg_ref[:, lanes(h)] = (vlocal[:, lanes(h)] + nn(kdec[:, lanes(h)], later)).astype(BF16)
+
+    scan_sent(1)
+
+
+def store(*refs):
+    *refs, sems = refs
+    count = len(refs) // 2
+    copies = [pltpu.make_async_copy(refs[i], refs[count + i], sems.at[i]) for i in range(count)]
+    for copy in copies:
+        copy.start()
+    for copy in copies:
         copy.wait()
-
-
-def store(*refs):
-    count = len(refs) // 2
-    for src, dst in zip(refs[:count], refs[count:]):
-        dst[...] = src[...]
 
 
 def on_device(chips, queries, keys, values, log_decay, gate, norm_gain, out_weight, target):
@@ -655,12 +683,6 @@
     vmem = pltpu.VMEM
     dma = pltpu.SemaphoreType.DMA
     scratch = [
-        vmem((rows, tokens), BF16),
-        vmem((tokens, width), BF16),
-        vmem((tokens, width), BF16),
-        vmem((tokens, width), BF16),
-        vmem((tokens, width), BF16),
-        dma((5,)),
         vmem((tokens, width), BF16),
         vmem((tokens, width), BF16),
         vmem((tokens, width), BF16),
@@ -686,6 +708,11 @@
         vmem((tokens, width), F32),
         vmem((tokens, width), F32),
         vmem((tokens, width), BF16),
+        vmem((width // DH, tokens, DH), F32),
+        vmem((width // DH, tokens, DH), F32),
+        vmem((tokens, width), BF16),
+        vmem((tokens, width), F32),
+        vmem((tokens, width), F32),
         vmem((8, 128), F32),
         vmem((8, 128), F32),
         vmem((Y, 8, 128), F32),
@@ -730,26 +757,26 @@
     ]
     in_vmem = pl.BlockSpec(memory_space=pltpu.VMEM)
     in_hbm = pl.BlockSpec(memory_space=pltpu.HBM)
-    wide = jax.ShapeDtypeStruct((tokens, width), BF16)
-    out_shape = (jax.ShapeDtypeStruct((rows, tokens), BF16), wide, wide, wide, wide)
+    shapes = [(rows, tokens)] + [(tokens, width)] * 4
+    operands = (queries, keys, values, log_decay.T, gate, norm_gain.reshape(1, width), out_weight, target.T)
     results = pl.pallas_call(
         functools.partial(kernel, chips),
-        out_shape=out_shape,
+        out_shape=tuple(pltpu.VMEM(shape, BF16) for shape in shapes),
         in_specs=[in_hbm] * 8,
-        out_specs=(in_hbm,) * 5,
+        out_specs=(in_vmem,) * 5,
         scratch_shapes=scratch,
         compiler_params=pltpu.CompilerParams(
-            collective_id=0, has_side_effects=True, vmem_limit_bytes=63 * 1024 * 1024
+            collective_id=0, has_side_effects=True, vmem_limit_bytes=48 * 1024 * 1024
         ),
         cost_estimate=pl.CostEstimate(flops=2 * 10**9, bytes_accessed=8 * 10**6, transcendentals=10**6),
         name="attention_layer",
-    )(queries, keys, values, log_decay.T, gate, norm_gain.reshape(1, width), out_weight, target.T)
+    )(*[pltpu.with_memory_space_constraint(operand, pltpu.HBM) for operand in operands])
     output, *grads = pl.pallas_call(
         store,
-        out_shape=out_shape,
+        out_shape=tuple(jax.ShapeDtypeStruct(shape, BF16) for shape in shapes),
         in_specs=[in_vmem] * 5,
-        out_specs=(in_vmem,) * 5,
-        compiler_params=pltpu.CompilerParams(vmem_limit_bytes=63 * 1024 * 1024),
+        out_specs=(in_hbm,) * 5,
+        scratch_shapes=[dma((5,))],
         name="store",
     )(*results)
     return (output.T, *grads)

time: 86.8 us -> 88.1 us (1.015)
  local copies, waits for them, and re-layouts: 0 us -> 3.22 us
  Pallas kernels: 86 us -> 84 us
    unnamed x0 -> x10, local copies, waits for them, and re-layouts: none -> 3.22 us
    pallas_call x2, Pallas kernels: 86 us -> 84 us  [the longest x1 82.1 us: on_device(): pl.pallas_call(functools.partial(kernel, chips), out_shape=tuple((pltpu.V...]
where the time goes in v5:
time: 88.1 us; the launch traced here: 87.9 us
  Pallas kernels  84 us (95%)
  local copies, waits for them, and re-layouts  3.22 us (4%)
    pallas_call x1, Pallas kernels, on_device(): pl.pallas_call(functools.partial(kernel, chips), out_shape=tuple((pltpu.V...  82.1 us
    unnamed x10, local copies, waits for them, and re-layouts  3.22 us
    pallas_call x1, Pallas kernels, on_device(): pl.pallas_call(store, out_shape=tuple((jax.ShapeDtypeStruct(shape, BF16)...  2 us

profile of v5, /device:TPU:1, one launch (start us, length us, event | category | flops | bytes accessed | tf_op | source)
XLA Modules:
  0.0 87.9 jit_solution(4020405168849080474)
XLA Ops:
  0.6 82.1 %attention_layer.1 = (bf16[192,256]{1,0:T(8,128)(2,1)S(1)}, bf16[256,256]{1,0:T(8,128)(2,1)S(1)}, bf16[256,256]{1,0:T(8,128)(2,1)S(1)}, bf16[256,256]{1,0:T(8,128)(2,1)S(1)}, bf16[256,256]{1,0:T(8,128)(2,1)S(1)}) custom-call(bf16[256,256]{1,0:T(8,128)(2,1)} %q_in.1, bf16[256,256]{1,0:T(8,128)(2,1)} %k_in.1, bf16[256,256]{1,0:T(8,128)(2,1)} %v_in.1, ...), custom_call_target="tpu_custom_call" | custom-call | flops 2000000000 | bytes 8000000 | tf_op jit(solution)/shard_map/attention_layer/pallas_call | solution.py:762
  82.7 0.0 copy-start
  82.7 0.6 copy-done
  83.3 0.0 copy-start.1
  83.3 0.6 copy-done.1
  84.0 0.0 copy-start.2
  84.0 0.6 copy-done.2
  84.6 0.0 copy-start.3
  84.6 0.6 copy-done.3
  85.3 0.0 copy-start.4
  85.3 0.6 copy-done.4
  85.9 2.0 %store.1 = (bf16[192,256]{1,0:T(8,128)(2,1)}, bf16[256,256]{1,0:T(8,128)(2,1)}, bf16[256,256]{1,0:T(8,128)(2,1)}, bf16[256,256]{1,0:T(8,128)(2,1)}, bf16[256,256]{1,0:T(8,128)(2,1)}) custom-call(bf16[192,256]{1,0:T(8,128)(2,1)} %copy-done.4, bf16[256,256]{1,0:T(8,128)(2,1)} %copy-done, bf16[256,256]{1,0:T(8,128)(2,1)} %copy-done.1, ...), custom_call_target="tpu_custom_call" | custom-call | tf_op jit(solution)/shard_map/store/pallas_call | solution.py:774
Async XLA Ops:
  82.7 0.6 copy-start
  83.3 0.6 copy-start.1
  84.0 0.6 copy-start.2
  84.6 0.7 copy-start.3
  85.3 0.6 copy-start.4

commit v6 on v5

--- a/solution.py
+++ b/solution.py
@@ -473,19 +473,21 @@
     for stage in stages:
         stage()
 
-    def y_start(part, kind, piece, value, device):
-        ystage[part, kind, piece] = value.astype(BF16)
+    steps = (2, 1, 3)
+
+    def y_start(part, step):
+        ystage[part, step - 1] = yacc[part, xs(step)].astype(BF16)
         send(
-            ystage.at[part, kind, piece],
-            yrecv.at[part, kind, piece],
-            y_send.at[part, kind, piece],
-            y_recv.at[part, kind, piece],
-            device,
+            ystage.at[part, step - 1],
+            yrecv.at[part, step - 1],
+            y_send.at[part, step - 1],
+            y_recv.at[part, step - 1],
+            at_x(step),
         )
 
-    def y_arrived(part, kind, piece):
-        arrived(yrecv.at[part, kind, piece], y_recv.at[part, kind, piece])
-        return yrecv[part, kind, piece].astype(F32)
+    def y_arrived(part, step):
+        arrived(yrecv.at[part, step - 1], y_recv.at[part, step - 1])
+        return yrecv[part, step - 1].astype(F32)
 
     for part in range(2):
         u_pass(far - 1, part)
@@ -494,51 +496,33 @@
 
         def finish(rows_of):
             block = wb[last, rows_of].reshape(rows, width)
-            yacc[part, rows_of] += nt(block, last_u).reshape(yacc.shape[2:])
-
-        finish(opp)
-        y_start(part, 0, 0, yacc[part, opp, 0], at_x(1))
-        y_start(part, 0, 1, yacc[part, opp, 1], at_x(-1))
-        finish(right)
-        y_start(part, 1, 1, yacc[part, right, 1], at_x(1))
-        finish(left)
-        y_start(part, 1, 0, yacc[part, left, 0], at_x(-1))
+            yacc[part, rows_of] += nt(block, last_u)
+
+        for step in steps:
+            finish(xs(step))
+            y_start(part, step)
         finish(x)
-    for part in range(2):
-        y_start(part, 2, 0, yacc[part, right, 0] + y_arrived(part, 0, 0), at_x(1))
-        y_start(part, 2, 1, yacc[part, left, 1] + y_arrived(part, 0, 1), at_x(-1))
 
     inv_rms = lax.rsqrt(small_sum(0) / total_features + EPS)
 
-    def g_start(part, source, piece, kind, device):
-        ref = gx.at[part, source, piece]
-        send(ref, ref, g_send.at[part, kind, piece], g_recv.at[part, kind, piece], device)
-
-    def g_arrived(part, source, piece, kind):
-        arrived(gx.at[part, source, piece], g_recv.at[part, kind, piece])
+    def g_arrived(part, step):
+        arrived(gx.at[part, xs(-step)], g_recv.at[part, step - 1])
 
     products = []
     for part in range(2):
         span = slice(part * half_tokens, (part + 1) * half_tokens)
-        product = jnp.zeros((1, half_tokens), F32)
-        for piece in range(2):
-            total = yacc[part, x, piece] + y_arrived(part, 1, piece) + y_arrived(part, 2, piece)
-            rounded = (total * inv_rms[:, span]).astype(BF16)
-            out_ref[piece * half : (piece + 1) * half, span] = rounded
-            wanted = target_ref[piece * half : (piece + 1) * half, span].astype(F32)
-            grad = (rounded.astype(F32) - wanted).astype(BF16)
-            gx[part, x, piece] = grad
-            g_start(part, x, piece, piece, at_x(1 - 2 * piece))
-            product = product + jnp.sum(grad.astype(F32) * total, axis=0, keepdims=True)
-        g_start(part, x, 1, 0, at_x(1))
-        g_start(part, x, 0, 1, at_x(-1))
-        products.append(product)
+        total = yacc[part, x]
+        for step in (1, 3, 2):
+            total = total + y_arrived(part, step)
+        rounded = (total * inv_rms[:, span]).astype(BF16)
+        grad = (rounded.astype(F32) - target_ref[:, span].astype(F32)).astype(BF16)
+        gx[part, x] = grad
+        for step in steps:
+            ref = gx.at[part, x]
+            send(ref, ref, g_send.at[part, step - 1], g_recv.at[part, step - 1], at_x(step))
+        out_ref[:, span] = rounded
+        products.append(jnp.sum(grad.astype(F32) * total, axis=0, keepdims=True))
     small_share(1, jnp.concatenate(products, axis=1))
-    for part in range(2):
-        g_arrived(part, left, 0, 0)
-        g_start(part, left, 0, 2, at_x(1))
-        g_arrived(part, right, 1, 1)
-        g_start(part, right, 1, 2, at_x(-1))
 
     eye = identity(half_tokens)
 
@@ -567,10 +551,8 @@
     for step in range(far):
         for part in range(2):
             if step == 0:
-                g_arrived(part, left, 1, 0)
-                g_arrived(part, right, 0, 1)
-                for piece in range(2):
-                    g_arrived(part, opp, piece, 2)
+                for x_step in (1, 3, 2):
+                    g_arrived(part, x_step)
                 gall[part] = nt(eye, gx[part].reshape(X * rows, half_tokens)).astype(BF16)
             sums = [
                 feature_part(zs(ways[way] * (hops[way] - step)), part) if step < hops[way] else None
@@ -627,10 +609,9 @@
                 for h in range(heads):
                     arrived(fstage.at[slot, part, h], f_send.at[slot, part, h])
     for part in range(2):
-        for kind in range(3):
-            for piece in range(2):
-                arrived(ystage.at[part, kind, piece], y_send.at[part, kind, piece])
-                arrived(ystage.at[part, kind, piece], g_send.at[part, kind, piece])
+        for slot in range(X - 1):
+            arrived(ystage.at[part, slot], y_send.at[part, slot])
+            arrived(ystage.at[part, slot], g_send.at[part, slot])
     arrived(bown, b_send)
     for distance in range(1, Y):
         arrived(bown, bc_send.at[distance - 1])
@@ -694,10 +675,10 @@
         vmem((Z, X, 2, half, width), BF16),
         vmem((Z, half, width), BF16),
         vmem((Z, 2, tokens // 2, width), BF16),
-        vmem((2, X, 2, half, tokens // 2), F32),
-        vmem((2, 3, 2, half, tokens // 2), BF16),
-        vmem((2, 3, 2, half, tokens // 2), BF16),
-        vmem((2, X, 2, half, tokens // 2), BF16),
+        vmem((2, X, rows, tokens // 2), F32),
+        vmem((2, X - 1, rows, tokens // 2), BF16),
+        vmem((2, X - 1, rows, tokens // 2), BF16),
+        vmem((2, X, rows, tokens // 2), BF16),
         vmem((2, tokens // 2, X * rows), BF16),
         vmem((Z - 1, 2, 2, tokens // 2, DH), BF16),
         vmem((Z - 1, 2, 2, tokens // 2, DH), BF16),
@@ -734,10 +715,10 @@
         dma((3,)),
         dma((2, far, 2)),
         dma((2, far, 2)),
-        dma((2, 3, 2)),
-        dma((2, 3, 2)),
-        dma((2, 3, 2)),
-        dma((2, 3, 2)),
+        dma((2, X - 1)),
+        dma((2, X - 1)),
+        dma((2, X - 1)),
+        dma((2, X - 1)),
         dma((Z - 1, 2, 2)),
         dma((Z - 1, 2, 2)),
         dma,
@@ -777,6 +758,7 @@
         in_specs=[in_vmem] * 5,
         out_specs=(in_hbm,) * 5,
         scratch_shapes=[dma((5,))],
+        compiler_params=pltpu.CompilerParams(vmem_limit_bytes=4 * 1024 * 1024),
         name="store",
     )(*results)
     return (output.T, *grads)

time: 88.1 us -> 82.2 us (0.933)
  local copies, waits for them, and re-layouts: 3.22 us -> 0 us
  Pallas kernels: 84 us -> 81.4 us
    unnamed x10 -> x0, local copies, waits for them, and re-layouts: 3.22 us -> none
    pallas_call x1, Pallas kernels: 82.1 us -> 80.5 us  [on_device(): pl.pallas_call(functools.partial(kernel, chips), out_shape=tuple((pltpu.V...]
    pallas_call x1, Pallas kernels: 2 us -> 0.86 us  [on_device(): pl.pallas_call(store, out_shape=tuple((jax.ShapeDtypeStruct(shape, BF16)...]
where the time goes in v6:
time: 82.2 us; the launch traced here: 82 us
  Pallas kernels  81.4 us (99%)
    pallas_call x1, Pallas kernels, on_device(): pl.pallas_call(functools.partial(kernel, chips), out_shape=tuple((pltpu.V...  80.5 us

profile of v6, /device:TPU:1, one launch (start us, length us, event | category | flops | bytes accessed | tf_op | source)
XLA Modules:
  0.0 82.0 jit_solution(8942314996970494758)
XLA Ops:
  0.6 80.5 %attention_layer.1 = (bf16[192,256]{1,0:T(8,128)(2,1)S(1)}, bf16[256,256]{1,0:T(8,128)(2,1)S(1)}, bf16[256,256]{1,0:T(8,128)(2,1)S(1)}, bf16[256,256]{1,0:T(8,128)(2,1)S(1)}, bf16[256,256]{1,0:T(8,128)(2,1)S(1)}) custom-call(bf16[256,256]{1,0:T(8,128)(2,1)} %q_in.1, bf16[256,256]{1,0:T(8,128)(2,1)} %k_in.1, bf16[256,256]{1,0:T(8,128)(2,1)} %v_in.1, ...), custom_call_target="tpu_custom_call" | custom-call | flops 2000000000 | bytes 8000000 | tf_op jit(solution)/shard_map/attention_layer/pallas_call | solution.py:743
  81.2 0.9 %store.1 = (bf16[192,256]{1,0:T(8,128)(2,1)}, bf16[256,256]{1,0:T(8,128)(2,1)}, bf16[256,256]{1,0:T(8,128)(2,1)}, bf16[256,256]{1,0:T(8,128)(2,1)}, bf16[256,256]{1,0:T(8,128)(2,1)}) custom-call(bf16[192,256]{1,0:T(8,128)(2,1)S(1)} %get-tuple-element.15.refs_0_, bf16[256,256]{1,0:T(8,128)(2,1)S(1)} %get-tuple-element.16.refs_1_, ...), custom_call_target="tpu_custom_call" | custom-call | tf_op jit(solution)/shard_map/store/pallas_call | solution.py:755

commit v7 on v6

--- a/solution.py
+++ b/solution.py
@@ -368,12 +368,12 @@
     hops = (far, near)
     ways = (sign, -sign)
 
-    def u_part(way, step, part):
-        return uall.at[zs(-ways[way] * step), part]
-
-    def u_start(way, step, part):
-        ref = u_part(way, step, part)
-        send(ref, ref, u_send.at[way, step, part], u_recv.at[way, step, part], at_z(ways[way]))
+    def u_part(way, step, part, h):
+        return uall.at[zs(-ways[way] * step), part, h]
+
+    def u_start(way, step, part, h):
+        ref = u_part(way, step, part, h)
+        send(ref, ref, u_send.at[way, step, part, h], u_recv.at[way, step, part, h], at_z(ways[way]))
 
     for part in range(2):
         span = slice(part * half_tokens, (part + 1) * half_tokens)
@@ -381,10 +381,10 @@
             from_state = nn(q_ref[span, lanes(h)], state[0, h]) * from_start[h, span, :]
             attended = att[span, lanes(h)] + from_state
             att[span, lanes(h)] = attended
-            uall[z, part, :, lanes(h)] = (attended * scale[span, lanes(h)]).astype(BF16)
-        for way in range(2):
-            if hops[way] > 0:
-                u_start(way, 0, part)
+            uall[z, part, h] = (attended * scale[span, lanes(h)]).astype(BF16)
+            for way in range(2):
+                if hops[way] > 0:
+                    u_start(way, 0, part, h)
 
     def small_share(turn, value):
         small_z[turn, 0] = value
@@ -423,15 +423,19 @@
     def w_block(block):
         return wb[block].reshape(X * rows, width)
 
+    def u_block(block, part):
+        return jnp.concatenate([uall[block, part, h] for h in range(heads)], axis=1)
+
     def accumulate(block, part):
-        yacc[part] += nt(w_block(block), uall[block, part]).reshape(yacc.shape[1:])
+        yacc[part] += nt(w_block(block), u_block(block, part)).reshape(yacc.shape[1:])
 
     def u_pass(step, part):
-        for way in range(2):
-            if step < hops[way]:
-                arrived(u_part(way, step + 1, part), u_recv.at[way, step, part])
-                if step + 1 < hops[way]:
-                    u_start(way, step + 1, part)
+        for h in range(heads):
+            for way in range(2):
+                if step < hops[way]:
+                    arrived(u_part(way, step + 1, part, h), u_recv.at[way, step, part, h])
+                    if step + 1 < hops[way]:
+                        u_start(way, step + 1, part, h)
 
     def absorb(step):
         for way in range(2):
@@ -439,39 +443,25 @@
                 for part in range(2):
                     accumulate(zs(-ways[way] * (step + 1)), part)
 
-    def w_first():
-        w_pair(left, w_recv.at[1], 0)
-        w_pair(right, w_recv.at[2], 1)
-
-    def w_second():
-        small_cross(0)
-        w_pair(opp, w_recv.at[3], 2)
-
-    def w_third():
-        for part in range(2):
-            arrived(wb.at[:, x, part], w_own)
-        for slot, source in enumerate((left, right, opp)):
-            arrived(wb.at[:, source, 1 - core], ws_recv.at[slot])
-        for part in range(2):
-            yacc[part] = nt(w_block(z), uall[z, part]).reshape(yacc.shape[1:])
-
-    stages = [w_first, w_second, w_third]
-    ready = 0
     for step in range(far - 1):
         for part in range(2):
             u_pass(step, part)
-        if step < len(stages) - 1:
-            stages[step]()
-        if step == len(stages) - 2 or step == far - 2:
-            for stage in stages[min(step, len(stages) - 2) + 1 :]:
-                stage()
-            stages = []
-        if not stages:
-            while ready <= step:
-                absorb(ready)
-                ready += 1
-    for stage in stages:
-        stage()
+        if step == far - 3:
+            w_pair(left, w_recv.at[1], 0)
+            w_pair(right, w_recv.at[2], 1)
+    if far < 3:
+        w_pair(left, w_recv.at[1], 0)
+        w_pair(right, w_recv.at[2], 1)
+    w_pair(opp, w_recv.at[3], 2)
+    small_cross(0)
+    for part in range(2):
+        arrived(wb.at[:, x, part], w_own)
+    for slot, source in enumerate((left, right, opp)):
+        arrived(wb.at[:, source, 1 - core], ws_recv.at[slot])
+    for part in range(2):
+        yacc[part] = nt(w_block(z), u_block(z, part)).reshape(yacc.shape[1:])
+    for step in range(far - 1):
+        absorb(step)
 
     steps = (2, 1, 3)
 
@@ -492,7 +482,7 @@
     for part in range(2):
         u_pass(far - 1, part)
         last = zs(sign * far)
-        last_u = uall[last, part]
+        last_u = u_block(last, part)
 
         def finish(rows_of):
             block = wb[last, rows_of].reshape(rows, width)
@@ -604,9 +594,9 @@
     for way in range(2):
         for step in range(hops[way]):
             for part in range(2):
-                arrived(u_part(way, step, part), u_send.at[way, step, part])
                 slot = f_slot(way, step)
                 for h in range(heads):
+                    arrived(u_part(way, step, part, h), u_send.at[way, step, part, h])
                     arrived(fstage.at[slot, part, h], f_send.at[slot, part, h])
     for part in range(2):
         for slot in range(X - 1):
@@ -674,7 +664,7 @@
         dma((7,)),
         vmem((Z, X, 2, half, width), BF16),
         vmem((Z, half, width), BF16),
-        vmem((Z, 2, tokens // 2, width), BF16),
+        vmem((Z, 2, width // DH, tokens // 2, DH), BF16),
         vmem((2, X, rows, tokens // 2), F32),
         vmem((2, X - 1, rows, tokens // 2), BF16),
         vmem((2, X - 1, rows, tokens // 2), BF16),
@@ -713,8 +703,8 @@
         dma,
         dma((3,)),
         dma((3,)),
-        dma((2, far, 2)),
-        dma((2, far, 2)),
+        dma((2, far, 2, 2)),
+        dma((2, far, 2, 2)),
         dma((2, X - 1)),
         dma((2, X - 1)),
         dma((2, X - 1)),

time: 82.2 us -> 82.5 us (level)
  no operation moved by 1% of the time
where the time goes in v7:
time: 82.5 us; the launch traced here: 82.1 us
  Pallas kernels  81.4 us (99%)
    pallas_call x1, Pallas kernels, on_device(): pl.pallas_call(functools.partial(kernel, chips), out_shape=tuple((pltpu.V...  80.6 us

profile of v7, /device:TPU:1, one launch (start us, length us, event | category | flops | bytes accessed | tf_op | source)
XLA Modules:
  0.0 82.1 jit_solution(2588900109803119476)
XLA Ops:
  0.6 80.6 %attention_layer.1 = (bf16[192,256]{1,0:T(8,128)(2,1)S(1)}, bf16[256,256]{1,0:T(8,128)(2,1)S(1)}, bf16[256,256]{1,0:T(8,128)(2,1)S(1)}, bf16[256,256]{1,0:T(8,128)(2,1)S(1)}, bf16[256,256]{1,0:T(8,128)(2,1)S(1)}) custom-call(bf16[256,256]{1,0:T(8,128)(2,1)} %q_in.1, bf16[256,256]{1,0:T(8,128)(2,1)} %k_in.1, bf16[256,256]{1,0:T(8,128)(2,1)} %v_in.1, ...), custom_call_target="tpu_custom_call" | custom-call | flops 2000000000 | bytes 8000000 | tf_op jit(solution)/shard_map/attention_layer/pallas_call | solution.py:733
  81.2 0.9 %store.1 = (bf16[192,256]{1,0:T(8,128)(2,1)}, bf16[256,256]{1,0:T(8,128)(2,1)}, bf16[256,256]{1,0:T(8,128)(2,1)}, bf16[256,256]{1,0:T(8,128)(2,1)}, bf16[256,256]{1,0:T(8,128)(2,1)}) custom-call(bf16[192,256]{1,0:T(8,128)(2,1)S(1)} %get-tuple-element.15.refs_0_, bf16[256,256]{1,0:T(8,128)(2,1)S(1)} %get-tuple-element.16.refs_1_, ...), custom_call_target="tpu_custom_call" | custom-call | tf_op jit(solution)/shard_map/store/pallas_call | solution.py:745

commit v8 on v6

--- a/solution.py
+++ b/solution.py
@@ -224,6 +224,10 @@
             ).start()
         return carry
 
+    pl.semaphore_wait(barrier, len(partners))
+    lax.fori_loop(0, Z, w_far, 0)
+    lax.fori_loop(0, Z, w_near, 0)
+
     row = lax.broadcasted_iota(jnp.int32, (tokens, tokens), 0)
     column = lax.broadcasted_iota(jnp.int32, (tokens, tokens), 1)
     causal = row >= column
@@ -326,12 +330,9 @@
     def scan_take(turn):
         arrived(state.at[turn, 1 - core], c_recv.at[turn])
 
-    pl.semaphore_wait(barrier, len(partners))
     send(bown, bsib, b_send, b_recv, sibling)
     for h in range(heads):
         scan_give(0, h, own[h])
-    lax.fori_loop(0, Z, w_far, 0)
-    lax.fori_loop(0, Z, w_near, 0)
     lax.fori_loop(0, Z, w_mine, 0)
 
     arrived(bsib, b_recv)
@@ -423,8 +424,16 @@
     def w_block(block):
         return wb[block].reshape(X * rows, width)
 
-    def accumulate(block, part):
-        yacc[part] += nt(w_block(block), uall[block, part]).reshape(yacc.shape[1:])
+    def w_rows(block, rows_of):
+        return wb[block, rows_of].reshape(rows, width)
+
+    def absorb(rows_of):
+        blocks = [z] + [zs(-ways[way] * (step + 1)) for step in range(far - 1) for way in range(2) if step < hops[way]]
+        for part in range(2):
+            total = nt(w_rows(z, rows_of), uall[z, part])
+            for block in blocks[1:]:
+                total = total + nt(w_rows(block, rows_of), uall[block, part])
+            yacc[part, rows_of] = total
 
     def u_pass(step, part):
         for way in range(2):
@@ -433,45 +442,23 @@
                 if step + 1 < hops[way]:
                     u_start(way, step + 1, part)
 
-    def absorb(step):
-        for way in range(2):
-            if step < hops[way]:
-                for part in range(2):
-                    accumulate(zs(-ways[way] * (step + 1)), part)
-
-    def w_first():
-        w_pair(left, w_recv.at[1], 0)
-        w_pair(right, w_recv.at[2], 1)
-
-    def w_second():
-        small_cross(0)
-        w_pair(opp, w_recv.at[3], 2)
-
-    def w_third():
-        for part in range(2):
-            arrived(wb.at[:, x, part], w_own)
-        for slot, source in enumerate((left, right, opp)):
-            arrived(wb.at[:, source, 1 - core], ws_recv.at[slot])
-        for part in range(2):
-            yacc[part] = nt(w_block(z), uall[z, part]).reshape(yacc.shape[1:])
-
-    stages = [w_first, w_second, w_third]
-    ready = 0
     for step in range(far - 1):
         for part in range(2):
             u_pass(step, part)
-        if step < len(stages) - 1:
-            stages[step]()
-        if step == len(stages) - 2 or step == far - 2:
-            for stage in stages[min(step, len(stages) - 2) + 1 :]:
-                stage()
-            stages = []
-        if not stages:
-            while ready <= step:
-                absorb(ready)
-                ready += 1
-    for stage in stages:
-        stage()
+        if step == max(far - 3, 0):
+            w_pair(left, w_recv.at[1], 0)
+            w_pair(right, w_recv.at[2], 1)
+    if far < 2:
+        w_pair(left, w_recv.at[1], 0)
+        w_pair(right, w_recv.at[2], 1)
+    for part in range(2):
+        arrived(wb.at[:, x, part], w_own)
+    absorb(x)
+    w_pair(opp, w_recv.at[3], 2)
+    for slot, source in enumerate((left, right, opp)):
+        arrived(wb.at[:, source, 1 - core], ws_recv.at[slot])
+        absorb(source)
+    small_cross(0)
 
     steps = (2, 1, 3)
 
@@ -495,8 +482,7 @@
         last_u = uall[last, part]
 
         def finish(rows_of):
-            block = wb[last, rows_of].reshape(rows, width)
-            yacc[part, rows_of] += nt(block, last_u)
+            yacc[part, rows_of] += nt(w_rows(last, rows_of), last_u)
 
         for step in steps:
             finish(xs(step))

time: 82.2 us -> 83.3 us (1.013)
  Pallas kernels: 81.4 us -> 82.5 us
    pallas_call x1, Pallas kernels: 80.5 us -> 81.7 us  [on_device(): pl.pallas_call(functools.partial(kernel, chips), out_shape=tuple((pltpu.V...]
where the time goes in v8:
time: 83.3 us; the launch traced here: 83.2 us
  Pallas kernels  82.5 us (99%)
    pallas_call x1, Pallas kernels, on_device(): pl.pallas_call(functools.partial(kernel, chips), out_shape=tuple((pltpu.V...  81.7 us

profile of v8, /device:TPU:1, one launch (start us, length us, event | category | flops | bytes accessed | tf_op | source)
XLA Modules:
  0.0 83.2 jit_solution(9683482028016540786)
XLA Ops:
  0.6 81.7 %attention_layer.1 = (bf16[192,256]{1,0:T(8,128)(2,1)S(1)}, bf16[256,256]{1,0:T(8,128)(2,1)S(1)}, bf16[256,256]{1,0:T(8,128)(2,1)S(1)}, bf16[256,256]{1,0:T(8,128)(2,1)S(1)}, bf16[256,256]{1,0:T(8,128)(2,1)S(1)}) custom-call(bf16[256,256]{1,0:T(8,128)(2,1)} %q_in.1, bf16[256,256]{1,0:T(8,128)(2,1)} %k_in.1, bf16[256,256]{1,0:T(8,128)(2,1)} %v_in.1, ...), custom_call_target="tpu_custom_call" | custom-call | flops 2000000000 | bytes 8000000 | tf_op jit(solution)/shard_map/attention_layer/pallas_call | solution.py:729
  82.3 0.9 %store.1 = (bf16[192,256]{1,0:T(8,128)(2,1)}, bf16[256,256]{1,0:T(8,128)(2,1)}, bf16[256,256]{1,0:T(8,128)(2,1)}, bf16[256,256]{1,0:T(8,128)(2,1)}, bf16[256,256]{1,0:T(8,128)(2,1)}) custom-call(bf16[192,256]{1,0:T(8,128)(2,1)S(1)} %get-tuple-element.15.refs_0_, bf16[256,256]{1,0:T(8,128)(2,1)S(1)} %get-tuple-element.16.refs_1_, ...), custom_call_target="tpu_custom_call" | custom-call | tf_op jit(solution)/shard_map/store/pallas_call | solution.py:741

commit v9 on v7

--- a/solution.py
+++ b/solution.py
@@ -319,9 +319,9 @@
         b_first = jnp.where(first_here, decays(bown), decays(bsib))
         carried = c_acc[...]
         after = jnp.exp(b_first) * carried + s_keep[turn]
-        state[turn, core] = jnp.where(first_here, carried, after).astype(BF16)
         c_out[turn] = jnp.where(first_here, after, carried).astype(BF16)
         send(c_out.at[turn], state.at[turn, core], c_send.at[turn], c_recv.at[turn], sibling)
+        state[turn, core] = jnp.where(first_here, carried, after).astype(BF16)
 
     def scan_take(turn):
         arrived(state.at[turn, 1 - core], c_recv.at[turn])
@@ -338,7 +338,7 @@
     bchip[y] = bown[...] + bsib[...]
     for distance in range(1, Y):
         place = lax.rem(y + distance, Y)
-        send(bchip.at[y], bchip.at[y], bc_send.at[distance - 1], bc_recv.at[distance - 1], at_y(place))
+        send(bchip.at[y], bchip.at[y], bc_send, bc_recv.at[distance - 1], at_y(place))
     scan_send(0)
 
     for load in loads[3:]:
@@ -350,19 +350,13 @@
         probs[h] = (nt(q_ref[:, lanes(h)], k_ref[:, lanes(h)]) * decay).astype(BF16)
         att[:, lanes(h)] = nn(probs[h], v_ref[:, lanes(h)])
         from_start[h] = jnp.exp(cums[h])
-        qdec[:, lanes(h)] = (q_ref[:, lanes(h)].astype(F32) * from_start[h]).astype(BF16)
         gate_open = jax.nn.sigmoid(gate_ref[:, lanes(h)].astype(F32))
         scale[:, lanes(h)] = gain_ref[:, lanes(h)] * gate_open
-        closed[:, lanes(h)] = 1.0 - gate_open
 
     for distance in range(1, Y):
         arrived(bchip.at[lax.rem(y - distance + Y, Y)], bc_recv.at[distance - 1])
 
-    arrived(wrelay, w_recv.at[0])
-    send(wrelay, wb.at[:, xs(-sign), core], w_send.at[3], w_recv.at[3], (ctx, z * X + x_far))
-
     scan_end(0)
-    scan_take(0)
 
     far, near = Z // 2, Z - 1 - Z // 2
     hops = (far, near)
@@ -373,15 +367,22 @@
 
     def u_start(way, step, part, h):
         ref = u_part(way, step, part, h)
-        send(ref, ref, u_send.at[way, step, part, h], u_recv.at[way, step, part, h], at_z(ways[way]))
-
-    for part in range(2):
-        span = slice(part * half_tokens, (part + 1) * half_tokens)
-        for h in range(heads):
-            from_state = nn(q_ref[span, lanes(h)], state[0, h]) * from_start[h, span, :]
-            attended = att[span, lanes(h)] + from_state
-            att[span, lanes(h)] = attended
-            uall[z, part, h] = (attended * scale[span, lanes(h)]).astype(BF16)
+        send(ref, ref, u_send, u_recv.at[way, step, part, h], at_z(ways[way]))
+
+    order = (core, 1 - core)
+
+    def any_lanes(h):
+        return pl.ds(pl.multiple_of(h * DH, DH), DH)
+
+    for turn, h in enumerate(order):
+        if turn == 1:
+            scan_take(0)
+        for part in range(2):
+            span = slice(part * half_tokens, (part + 1) * half_tokens)
+            from_state = nn(q_ref[span, any_lanes(h)], state[0, h]) * from_start[h, span, :]
+            attended = att[span, any_lanes(h)] + from_state
+            att[span, any_lanes(h)] = attended
+            uall[z, part, h] = (attended * scale[span, any_lanes(h)]).astype(BF16)
             for way in range(2):
                 if hops[way] > 0:
                     u_start(way, 0, part, h)
@@ -389,7 +390,7 @@
     def small_share(turn, value):
         small_z[turn, 0] = value
         for step in range(1, Z):
-            send(small_z.at[turn, 0], small_z.at[turn, step], sz_send.at[turn, step - 1], sz_recv.at[turn, step - 1], at_z(step))
+            send(small_z.at[turn, 0], small_z.at[turn, step], sz_send, sz_recv.at[turn, step - 1], at_z(step))
 
     def small_cross(turn):
         for step in range(1, Z):
@@ -399,7 +400,7 @@
             sum_z = sum_z + small_z[turn, step]
         small_x[turn, 0] = sum_z
         for step in range(1, X):
-            send(small_x.at[turn, 0], small_x.at[turn, step], sx_send.at[turn, step - 1], sx_recv.at[turn, step - 1], at_x(step))
+            send(small_x.at[turn, 0], small_x.at[turn, step], sx_send, sx_recv.at[turn, step - 1], at_x(step))
 
     def small_sum(turn):
         for step in range(1, X):
@@ -415,6 +416,13 @@
         squares = squares + jnp.sum(attended * attended, axis=1, keepdims=True)
     small_share(0, as_row(squares))
 
+    arrived(wrelay, w_recv.at[0])
+    send(wrelay, wb.at[:, xs(-sign), core], w_send.at[3], w_recv.at[3], (ctx, z * X + x_far))
+
+    for h in range(heads):
+        qdec[:, lanes(h)] = (q_ref[:, lanes(h)].astype(F32) * from_start[h]).astype(BF16)
+        closed[:, lanes(h)] = 1.0 - jax.nn.sigmoid(gate_ref[:, lanes(h)].astype(F32))
+
     def w_pair(source, sem, slot):
         ref = wb.at[:, source, core]
         arrived(ref, sem)
@@ -429,8 +437,8 @@
     def accumulate(block, part):
         yacc[part] += nt(w_block(block), u_block(block, part)).reshape(yacc.shape[1:])
 
-    def u_pass(step, part):
-        for h in range(heads):
+    def u_pass(step, part, some):
+        for h in some:
             for way in range(2):
                 if step < hops[way]:
                     arrived(u_part(way, step + 1, part, h), u_recv.at[way, step, part, h])
@@ -444,8 +452,9 @@
                     accumulate(zs(-ways[way] * (step + 1)), part)
 
     for step in range(far - 1):
-        for part in range(2):
-            u_pass(step, part)
+        for h in order:
+            for part in range(2):
+                u_pass(step, part, (h,))
         if step == far - 3:
             w_pair(left, w_recv.at[1], 0)
             w_pair(right, w_recv.at[2], 1)
@@ -470,7 +479,7 @@
         send(
             ystage.at[part, step - 1],
             yrecv.at[part, step - 1],
-            y_send.at[part, step - 1],
+            y_send,
             y_recv.at[part, step - 1],
             at_x(step),
         )
@@ -480,7 +489,7 @@
         return yrecv[part, step - 1].astype(F32)
 
     for part in range(2):
-        u_pass(far - 1, part)
+        u_pass(far - 1, part, order)
         last = zs(sign * far)
         last_u = u_block(last, part)
 
@@ -509,7 +518,7 @@
         gx[part, x] = grad
         for step in steps:
             ref = gx.at[part, x]
-            send(ref, ref, g_send.at[part, step - 1], g_recv.at[part, step - 1], at_x(step))
+            send(ref, ref, g_send, g_recv.at[part, step - 1], at_x(step))
         out_ref[:, span] = rounded
         products.append(jnp.sum(grad.astype(F32) * total, axis=0, keepdims=True))
     small_share(1, jnp.concatenate(products, axis=1))
@@ -528,7 +537,7 @@
         send(
             fstage.at[slot, part, h],
             frecv.at[slot, part, h],
-            f_send.at[slot, part, h],
+            f_send,
             f_recv.at[slot, part, h],
             at_z(ways[way]),
         )
@@ -591,26 +600,17 @@
         arrived(wrelay, w_send.at[index])
     for index in range(3):
         arrived(wrelay, ws_send.at[index])
-    for way in range(2):
-        for step in range(hops[way]):
-            for part in range(2):
-                slot = f_slot(way, step)
-                for h in range(heads):
-                    arrived(u_part(way, step, part, h), u_send.at[way, step, part, h])
-                    arrived(fstage.at[slot, part, h], f_send.at[slot, part, h])
-    for part in range(2):
-        for slot in range(X - 1):
-            arrived(ystage.at[part, slot], y_send.at[part, slot])
-            arrived(ystage.at[part, slot], g_send.at[part, slot])
+    arrived(uall.at[pl.ds(0, Z - 1)], u_send)
+    arrived(fstage, f_send)
+    arrived(ystage, y_send)
+    arrived(ystage, g_send)
     arrived(bown, b_send)
-    for distance in range(1, Y):
-        arrived(bown, bc_send.at[distance - 1])
+    if Y > 1:
+        arrived(bchip.at[pl.ds(0, Y - 1)], bc_send)
+    arrived(small_z.at[:, pl.ds(0, Z - 1)], sz_send)
+    arrived(small_x.at[:, pl.ds(0, X - 1)], sx_send)
     for turn in range(2):
         arrived(s_out.at[turn], s_send.at[turn])
-        for distance in range(1, Z):
-            arrived(small_z.at[turn, 0], sz_send.at[turn, distance - 1])
-        for distance in range(1, X):
-            arrived(small_x.at[turn, 0], sx_send.at[turn, distance - 1])
 
     def scan_sent(turn):
         arrived(c_out.at[turn], c_send.at[turn])
@@ -624,13 +624,13 @@
     scan_sent(0)
 
     scan_end(1)
-    scan_take(1)
-    for h in range(heads):
+    for turn, h in enumerate(order):
+        if turn == 1:
+            scan_take(1)
+        at = any_lanes(h)
         later = state[1, h]
-        kg_ref[:, lanes(h)] = (
-            klocal[:, lanes(h)] + until_end[h] * nt(v_ref[:, lanes(h)], later)
-        ).astype(BF16)
-        vg_ref[:, lanes(h)] = (vlocal[:, lanes(h)] + nn(kdec[:, lanes(h)], later)).astype(BF16)
+        kg_ref[:, at] = (klocal[:, at] + until_end[h] * nt(v_ref[:, at], later)).astype(BF16)
+        vg_ref[:, at] = (vlocal[:, at] + nn(kdec[:, at], later)).astype(BF16)
 
     scan_sent(1)
 
@@ -703,17 +703,17 @@
         dma,
         dma((3,)),
         dma((3,)),
+        dma,
         dma((2, far, 2, 2)),
-        dma((2, far, 2, 2)),
+        dma,
         dma((2, X - 1)),
+        dma,
         dma((2, X - 1)),
-        dma((2, X - 1)),
-        dma((2, X - 1)),
+        dma,
         dma((Z - 1, 2, 2)),
-        dma((Z - 1, 2, 2)),
-        dma,
-        dma,
-        dma((max(Y - 1, 1),)),
+        dma,
+        dma,
+        dma,
         dma((max(Y - 1, 1),)),
         dma((2,)),
         dma((2,)),
@@ -721,9 +721,9 @@
         dma((2, max(Y - 1, 1))),
         dma((2,)),
         dma((2,)),
+        dma,
         dma((2, Z - 1)),
-        dma((2, Z - 1)),
-        dma((2, X - 1)),
+        dma,
         dma((2, X - 1)),
     ]
     in_vmem = pl.BlockSpec(memory_space=pltpu.VMEM)

time: 82.5 us -> 80.2 us (0.972)
  Pallas kernels: 81.4 us -> 79.4 us
    pallas_call x1, Pallas kernels: 80.6 us -> 78.5 us  [on_device(): pl.pallas_call(functools.partial(kernel, chips), out_shape=tuple((pltpu.V...]
where the time goes in v9:
time: 80.2 us; the launch traced here: 80 us
  Pallas kernels  79.4 us (99%)
    pallas_call x1, Pallas kernels, on_device(): pl.pallas_call(functools.partial(kernel, chips), out_shape=tuple((pltpu.V...  78.5 us

profile of v9, /device:TPU:1, one launch (start us, length us, event | category | flops | bytes accessed | tf_op | source)
XLA Modules:
  0.0 80.0 jit_solution(7709768319220891693)
XLA Ops:
  0.6 78.5 %attention_layer.1 = (bf16[192,256]{1,0:T(8,128)(2,1)S(1)}, bf16[256,256]{1,0:T(8,128)(2,1)S(1)}, bf16[256,256]{1,0:T(8,128)(2,1)S(1)}, bf16[256,256]{1,0:T(8,128)(2,1)S(1)}, bf16[256,256]{1,0:T(8,128)(2,1)S(1)}) custom-call(bf16[256,256]{1,0:T(8,128)(2,1)} %q_in.1, bf16[256,256]{1,0:T(8,128)(2,1)} %k_in.1, bf16[256,256]{1,0:T(8,128)(2,1)} %v_in.1, ...), custom_call_target="tpu_custom_call" | custom-call | flops 2000000000 | bytes 8000000 | tf_op jit(solution)/shard_map/attention_layer/pallas_call | solution.py:733
  79.2 0.9 %store.1 = (bf16[192,256]{1,0:T(8,128)(2,1)}, bf16[256,256]{1,0:T(8,128)(2,1)}, bf16[256,256]{1,0:T(8,128)(2,1)}, bf16[256,256]{1,0:T(8,128)(2,1)}, bf16[256,256]{1,0:T(8,128)(2,1)}) custom-call(bf16[192,256]{1,0:T(8,128)(2,1)S(1)} %get-tuple-element.15.refs_0_, bf16[256,256]{1,0:T(8,128)(2,1)S(1)} %get-tuple-element.16.refs_1_, ...), custom_call_target="tpu_custom_call" | custom-call | tf_op jit(solution)/shard_map/store/pallas_call | solution.py:745

commit v10 on v9

--- a/solution.py
+++ b/solution.py
@@ -247,23 +247,21 @@
     def lanes(h):
         return slice(h * DH, (h + 1) * DH)
 
-    own = []
     for h in range(heads):
         until_end[h] = jnp.exp(totals[h] - cums[h])
-        decayed = (k_ref[:, lanes(h)].astype(F32) * until_end[h]).astype(BF16)
-        kdec[:, lanes(h)] = decayed
-        own.append(tn(decayed, v_ref[:, lanes(h)]))
+    order = (core, 1 - core)
+    others = (1 - core, core)
+
+    def any_lanes(h):
+        return pl.ds(pl.multiple_of(h * DH, DH), DH)
 
     def of_core(pair):
         return jnp.where(is_zero, pair[0], pair[1])
 
-    def scan_give(turn, h, value):
-        @pl.when(core == h)
-        def _():
+    def scan_give(turn, mine, value):
+        if mine:
             s_keep[turn] = value
-
-        @pl.when(core != h)
-        def _():
+        else:
             s_out[turn] = value.astype(BF16)
             send(s_out.at[turn], s_in.at[turn], s_send.at[turn], s_recv.at[turn], sibling)
 
@@ -328,8 +326,11 @@
 
     pl.semaphore_wait(barrier, len(partners))
     send(bown, bsib, b_send, b_recv, sibling)
-    for h in range(heads):
-        scan_give(0, h, own[h])
+    for mine, h in enumerate(others):
+        at = any_lanes(h)
+        decayed = (k_ref[:, at].astype(F32) * until_end[h]).astype(BF16)
+        kdec[:, at] = decayed
+        scan_give(0, mine, tn(decayed, v_ref[:, at]))
     lax.fori_loop(0, Z, w_far, 0)
     lax.fori_loop(0, Z, w_near, 0)
     lax.fori_loop(0, Z, w_mine, 0)
@@ -368,11 +369,6 @@
     def u_start(way, step, part, h):
         ref = u_part(way, step, part, h)
         send(ref, ref, u_send, u_recv.at[way, step, part, h], at_z(ways[way]))
-
-    order = (core, 1 - core)
-
-    def any_lanes(h):
-        return pl.ds(pl.multiple_of(h * DH, DH), DH)
 
     for turn, h in enumerate(order):
         if turn == 1:
@@ -547,44 +543,53 @@
         arrived(frecv.at[slot, part, h], f_recv.at[slot, part, h])
         return frecv[slot, part, h].astype(F32)
 
-    for step in range(far):
+    def by_head(value):
+        first, second = value[:, lanes(0)], value[:, lanes(1)]
+        return jnp.where(is_zero, second, first), jnp.where(is_zero, first, second)
+
+    for part in range(2):
+        for x_step in (1, 3, 2):
+            g_arrived(part, x_step)
+        gall[part] = nt(eye, gx[part].reshape(X * rows, half_tokens)).astype(BF16)
+        sums = [by_head(feature_part(zs(ways[way] * hops[way]), part)) if hops[way] > 0 else None for way in range(2)]
+        for turn in range(heads):
+            for way in range(2):
+                if hops[way] > 0:
+                    f_start(way, 0, part, turn, sums[way][turn])
+    small_cross(1)
+
+    def feature_both(block):
+        return by_head(nn(gall[...].reshape(tokens, X * rows), w_block(block)))
+
+    for step in range(1, far):
+        sums = [feature_both(zs(ways[way] * (hops[way] - step))) if step < hops[way] else None for way in range(2)]
         for part in range(2):
-            if step == 0:
-                for x_step in (1, 3, 2):
-                    g_arrived(part, x_step)
-                gall[part] = nt(eye, gx[part].reshape(X * rows, half_tokens)).astype(BF16)
-            sums = [
-                feature_part(zs(ways[way] * (hops[way] - step)), part) if step < hops[way] else None
-                for way in range(2)
-            ]
-            for h in range(heads):
+            span = slice(part * half_tokens, (part + 1) * half_tokens)
+            for turn in range(heads):
                 for way in range(2):
                     if step < hops[way]:
-                        value = sums[way][:, lanes(h)]
-                        if step > 0:
-                            value = value + f_arrived(way, step - 1, part, h)
-                        f_start(way, step, part, h, value)
-        if step == 0:
-            small_cross(1)
-
-    own_feature = [feature_part(z, part) for part in range(2)]
+                        value = sums[way][turn][span, :] + f_arrived(way, step - 1, part, turn)
+                        f_start(way, step, part, turn, value)
+
+    own_feature = feature_both(z)
     mean_product = as_columns(small_sum(1) / total_features)
     inv = as_columns(inv_rms)
 
-    for h in range(heads):
+    for turn, h in enumerate(others):
+        at = any_lanes(h)
         pieces = []
         for part in range(2):
-            value = own_feature[part][:, lanes(h)]
+            value = own_feature[turn][part * half_tokens : (part + 1) * half_tokens, :]
             for way in range(2):
                 if hops[way] > 0:
-                    value = value + f_arrived(way, hops[way] - 1, part, h)
+                    value = value + f_arrived(way, hops[way] - 1, part, turn)
             pieces.append(value)
-        attended = att[:, lanes(h)]
-        normed_grad = jnp.concatenate(pieces, axis=0) * scale[:, lanes(h)]
+        attended = att[:, at]
+        normed_grad = jnp.concatenate(pieces, axis=0) * scale[:, at]
         grad = (inv * normed_grad - inv * inv * inv * attended * mean_product).astype(BF16)
-        agrad[:, lanes(h)] = grad
-        scan_give(1, h, tn(qdec[:, lanes(h)], grad))
-        gg_ref[:, lanes(h)] = (normed_grad * attended * inv * closed[:, lanes(h)]).astype(BF16)
+        agrad[:, at] = grad
+        scan_give(1, turn, tn(qdec[:, at], grad))
+        gg_ref[:, at] = (normed_grad * attended * inv * closed[:, at]).astype(BF16)
 
     for h in range(heads):
         grad = agrad[:, lanes(h)]
@@ -613,7 +618,6 @@
         arrived(s_out.at[turn], s_send.at[turn])
 
     def scan_sent(turn):
-        arrived(c_out.at[turn], c_send.at[turn])
         step, _ = scan_way(turn)
         for distance in range(1, Y):
 
@@ -622,17 +626,19 @@
                 arrived(t_out.at[turn], t_send.at[turn, distance - 1])
 
     scan_sent(0)
+    arrived(c_out.at[0], c_send.at[0])
 
     scan_end(1)
     for turn, h in enumerate(order):
         if turn == 1:
+            scan_sent(1)
             scan_take(1)
         at = any_lanes(h)
         later = state[1, h]
         kg_ref[:, at] = (klocal[:, at] + until_end[h] * nt(v_ref[:, at], later)).astype(BF16)
         vg_ref[:, at] = (vlocal[:, at] + nn(kdec[:, at], later)).astype(BF16)
 
-    scan_sent(1)
+    arrived(c_out.at[1], c_send.at[1])
 
 
 def store(*refs):

time: 80.2 us -> 79.4 us (0.990)
    pallas_call x1, Pallas kernels: 78.5 us -> 77.7 us  [on_device(): pl.pallas_call(functools.partial(kernel, chips), out_shape=tuple((pltpu.V...]
where the time goes in v10:
time: 79.4 us; the launch traced here: 79.2 us
  Pallas kernels  78.6 us (99%)
    pallas_call x1, Pallas kernels, on_device(): pl.pallas_call(functools.partial(kernel, chips), out_shape=tuple((pltpu.V...  77.7 us

profile of v10, /device:TPU:1, one launch (start us, length us, event | category | flops | bytes accessed | tf_op | source)
XLA Modules:
  0.0 79.2 jit_solution(17734437006545718126)
XLA Ops:
  0.6 77.7 %attention_layer.1 = (bf16[192,256]{1,0:T(8,128)(2,1)S(1)}, bf16[256,256]{1,0:T(8,128)(2,1)S(1)}, bf16[256,256]{1,0:T(8,128)(2,1)S(1)}, bf16[256,256]{1,0:T(8,128)(2,1)S(1)}, bf16[256,256]{1,0:T(8,128)(2,1)S(1)}) custom-call(bf16[256,256]{1,0:T(8,128)(2,1)} %q_in.1, bf16[256,256]{1,0:T(8,128)(2,1)} %k_in.1, bf16[256,256]{1,0:T(8,128)(2,1)} %v_in.1, ...), custom_call_target="tpu_custom_call" | custom-call | flops 2000000000 | bytes 8000000 | tf_op jit(solution)/shard_map/attention_layer/pallas_call | solution.py:739
  78.4 0.9 %store.1 = (bf16[192,256]{1,0:T(8,128)(2,1)}, bf16[256,256]{1,0:T(8,128)(2,1)}, bf16[256,256]{1,0:T(8,128)(2,1)}, bf16[256,256]{1,0:T(8,128)(2,1)}, bf16[256,256]{1,0:T(8,128)(2,1)}) custom-call(bf16[192,256]{1,0:T(8,128)(2,1)S(1)} %get-tuple-element.15.refs_0_, bf16[256,256]{1,0:T(8,128)(2,1)S(1)} %get-tuple-element.16.refs_1_, ...), custom_call_target="tpu_custom_call" | custom-call | tf_op jit(solution)/shard_map/store/pallas_call | solution.py:751

commit v11 on v10

--- a/solution.py
+++ b/solution.py
@@ -447,18 +447,20 @@
                 for part in range(2):
                     accumulate(zs(-ways[way] * (step + 1)), part)
 
+    def w_forward():
+        small_cross(0)
+        w_pair(left, w_recv.at[1], 0)
+        w_pair(right, w_recv.at[2], 1)
+        w_pair(opp, w_recv.at[3], 2)
+
     for step in range(far - 1):
+        if step == far - 2:
+            w_forward()
         for h in order:
             for part in range(2):
                 u_pass(step, part, (h,))
-        if step == far - 3:
-            w_pair(left, w_recv.at[1], 0)
-            w_pair(right, w_recv.at[2], 1)
-    if far < 3:
-        w_pair(left, w_recv.at[1], 0)
-        w_pair(right, w_recv.at[2], 1)
-    w_pair(opp, w_recv.at[3], 2)
-    small_cross(0)
+    if far < 2:
+        w_forward()
     for part in range(2):
         arrived(wb.at[:, x, part], w_own)
     for slot, source in enumerate((left, right, opp)):

time: 79.4 us -> 78.9 us (level)
  no operation moved by 1% of the time
where the time goes in v11:
time: 78.9 us; the launch traced here: 78.8 us
  Pallas kernels  78.1 us (99%)
    pallas_call x1, Pallas kernels, on_device(): pl.pallas_call(functools.partial(kernel, chips), out_shape=tuple((pltpu.V...  77.3 us

profile of v11, /device:TPU:1, one launch (start us, length us, event | category | flops | bytes accessed | tf_op | source)
XLA Modules:
  0.0 78.8 jit_solution(8829576443037750386)
XLA Ops:
  0.6 77.3 %attention_layer.1 = (bf16[192,256]{1,0:T(8,128)(2,1)S(1)}, bf16[256,256]{1,0:T(8,128)(2,1)S(1)}, bf16[256,256]{1,0:T(8,128)(2,1)S(1)}, bf16[256,256]{1,0:T(8,128)(2,1)S(1)}, bf16[256,256]{1,0:T(8,128)(2,1)S(1)}) custom-call(bf16[256,256]{1,0:T(8,128)(2,1)} %q_in.1, bf16[256,256]{1,0:T(8,128)(2,1)} %k_in.1, bf16[256,256]{1,0:T(8,128)(2,1)} %v_in.1, ...), custom_call_target="tpu_custom_call" | custom-call | flops 2000000000 | bytes 8000000 | tf_op jit(solution)/shard_map/attention_layer/pallas_call | solution.py:741
  77.9 0.9 %store.1 = (bf16[192,256]{1,0:T(8,128)(2,1)}, bf16[256,256]{1,0:T(8,128)(2,1)}, bf16[256,256]{1,0:T(8,128)(2,1)}, bf16[256,256]{1,0:T(8,128)(2,1)}, bf16[256,256]{1,0:T(8,128)(2,1)}) custom-call(bf16[192,256]{1,0:T(8,128)(2,1)S(1)} %get-tuple-element.15.refs_0_, bf16[256,256]{1,0:T(8,128)(2,1)S(1)} %get-tuple-element.16.refs_1_, ...), custom_call_target="tpu_custom_call" | custom-call | tf_op jit(solution)/shard_map/store/pallas_call | solution.py:753

commit v12 on v11

--- a/solution.py
+++ b/solution.py
@@ -333,7 +333,6 @@
         scan_give(0, mine, tn(decayed, v_ref[:, at]))
     lax.fori_loop(0, Z, w_far, 0)
     lax.fori_loop(0, Z, w_near, 0)
-    lax.fori_loop(0, Z, w_mine, 0)
 
     arrived(bsib, b_recv)
     bchip[y] = bown[...] + bsib[...]
@@ -411,6 +410,7 @@
         attended = att[:, lanes(h)]
         squares = squares + jnp.sum(attended * attended, axis=1, keepdims=True)
     small_share(0, as_row(squares))
+    lax.fori_loop(0, Z, w_mine, 0)
 
     arrived(wrelay, w_recv.at[0])
     send(wrelay, wb.at[:, xs(-sign), core], w_send.at[3], w_recv.at[3], (ctx, z * X + x_far))
@@ -430,8 +430,9 @@
     def u_block(block, part):
         return jnp.concatenate([uall[block, part, h] for h in range(heads)], axis=1)
 
-    def accumulate(block, part):
-        yacc[part] += nt(w_block(block), u_block(block, part)).reshape(yacc.shape[1:])
+    def product(block):
+        both = nt(w_block(block), jnp.concatenate([u_block(block, part) for part in range(2)], axis=0))
+        return [both[:, part * half_tokens : (part + 1) * half_tokens].reshape(yacc.shape[1:]) for part in range(2)]
 
     def u_pass(step, part, some):
         for h in some:
@@ -444,8 +445,8 @@
     def absorb(step):
         for way in range(2):
             if step < hops[way]:
-                for part in range(2):
-                    accumulate(zs(-ways[way] * (step + 1)), part)
+                for part, value in enumerate(product(zs(-ways[way] * (step + 1)))):
+                    yacc[part] += value
 
     def w_forward():
         small_cross(0)
@@ -465,8 +466,8 @@
         arrived(wb.at[:, x, part], w_own)
     for slot, source in enumerate((left, right, opp)):
         arrived(wb.at[:, source, 1 - core], ws_recv.at[slot])
-    for part in range(2):
-        yacc[part] = nt(w_block(z), u_block(z, part)).reshape(yacc.shape[1:])
+    for part, value in enumerate(product(z)):
+        yacc[part] = value
     for step in range(far - 1):
         absorb(step)
 

time: 78.9 us -> 78.8 us (level)
  no operation moved by 1% of the time
where the time goes in v12:
time: 78.8 us; the launch traced here: 78.7 us
  Pallas kernels  78.1 us (99%)
    pallas_call x1, Pallas kernels, on_device(): pl.pallas_call(functools.partial(kernel, chips), out_shape=tuple((pltpu.V...  77.2 us

profile of v12, /device:TPU:1, one launch (start us, length us, event | category | flops | bytes accessed | tf_op | source)
XLA Modules:
  0.0 78.7 jit_solution(14133907088496459290)
XLA Ops:
  0.6 77.2 %attention_layer.1 = (bf16[192,256]{1,0:T(8,128)(2,1)S(1)}, bf16[256,256]{1,0:T(8,128)(2,1)S(1)}, bf16[256,256]{1,0:T(8,128)(2,1)S(1)}, bf16[256,256]{1,0:T(8,128)(2,1)S(1)}, bf16[256,256]{1,0:T(8,128)(2,1)S(1)}) custom-call(bf16[256,256]{1,0:T(8,128)(2,1)} %q_in.1, bf16[256,256]{1,0:T(8,128)(2,1)} %k_in.1, bf16[256,256]{1,0:T(8,128)(2,1)} %v_in.1, ...), custom_call_target="tpu_custom_call" | custom-call | flops 2000000000 | bytes 8000000 | tf_op jit(solution)/shard_map/attention_layer/pallas_call | solution.py:742
  77.8 0.9 %store.1 = (bf16[192,256]{1,0:T(8,128)(2,1)}, bf16[256,256]{1,0:T(8,128)(2,1)}, bf16[256,256]{1,0:T(8,128)(2,1)}, bf16[256,256]{1,0:T(8,128)(2,1)}, bf16[256,256]{1,0:T(8,128)(2,1)}) custom-call(bf16[192,256]{1,0:T(8,128)(2,1)S(1)} %get-tuple-element.15.refs_0_, bf16[256,256]{1,0:T(8,128)(2,1)S(1)} %get-tuple-element.16.refs_1_, ...), custom_call_target="tpu_custom_call" | custom-call | tf_op jit(solution)/shard_map/store/pallas_call | solution.py:754

commit v13 on v12

--- a/solution.py
+++ b/solution.py
@@ -335,11 +335,11 @@
     lax.fori_loop(0, Z, w_near, 0)
 
     arrived(bsib, b_recv)
+    scan_send(0)
     bchip[y] = bown[...] + bsib[...]
     for distance in range(1, Y):
         place = lax.rem(y + distance, Y)
         send(bchip.at[y], bchip.at[y], bc_send, bc_recv.at[distance - 1], at_y(place))
-    scan_send(0)
 
     for load in loads[3:]:
         load.wait()
@@ -578,6 +578,7 @@
     mean_product = as_columns(small_sum(1) / total_features)
     inv = as_columns(inv_rms)
 
+    normed_grads = []
     for turn, h in enumerate(others):
         at = any_lanes(h)
         pieces = []
@@ -592,13 +593,15 @@
         grad = (inv * normed_grad - inv * inv * inv * attended * mean_product).astype(BF16)
         agrad[:, at] = grad
         scan_give(1, turn, tn(qdec[:, at], grad))
-        gg_ref[:, at] = (normed_grad * attended * inv * closed[:, at]).astype(BF16)
+        normed_grads.append(normed_grad)
+    scan_send(1)
+    for turn, h in enumerate(others):
+        at = any_lanes(h)
+        gg_ref[:, at] = (normed_grads[turn] * att[:, at] * inv * closed[:, at]).astype(BF16)
 
     for h in range(heads):
         grad = agrad[:, lanes(h)]
         score_grad = (nt(grad, v_ref[:, lanes(h)]) * weight[h]).astype(BF16)
-        if h == 0:
-            scan_send(1)
         qg_ref[:, lanes(h)] = (
             nn(score_grad, k_ref[:, lanes(h)]) + from_start[h] * nt(grad, state[0, h])
         ).astype(BF16)

time: 78.8 us -> 80.3 us (1.019)
    pallas_call x1, Pallas kernels: 77.2 us -> 78.1 us  [on_device(): pl.pallas_call(functools.partial(kernel, chips), out_shape=tuple((pltpu.V...]
where the time goes in v13:
time: 80.3 us; the launch traced here: 79.6 us
  Pallas kernels  78.9 us (98%)
    pallas_call x1, Pallas kernels, on_device(): pl.pallas_call(functools.partial(kernel, chips), out_shape=tuple((pltpu.V...  78.1 us

profile of v13, /device:TPU:1, one launch (start us, length us, event | category | flops | bytes accessed | tf_op | source)
XLA Modules:
  0.0 79.6 jit_solution(11412476905761269779)
XLA Ops:
  0.6 78.1 %attention_layer.1 = (bf16[192,256]{1,0:T(8,128)(2,1)S(1)}, bf16[256,256]{1,0:T(8,128)(2,1)S(1)}, bf16[256,256]{1,0:T(8,128)(2,1)S(1)}, bf16[256,256]{1,0:T(8,128)(2,1)S(1)}, bf16[256,256]{1,0:T(8,128)(2,1)S(1)}) custom-call(bf16[256,256]{1,0:T(8,128)(2,1)} %q_in.1, bf16[256,256]{1,0:T(8,128)(2,1)} %k_in.1, bf16[256,256]{1,0:T(8,128)(2,1)} %v_in.1, ...), custom_call_target="tpu_custom_call" | custom-call | flops 2000000000 | bytes 8000000 | tf_op jit(solution)/shard_map/attention_layer/pallas_call | solution.py:745
  78.7 0.9 %store.1 = (bf16[192,256]{1,0:T(8,128)(2,1)}, bf16[256,256]{1,0:T(8,128)(2,1)}, bf16[256,256]{1,0:T(8,128)(2,1)}, bf16[256,256]{1,0:T(8,128)(2,1)}, bf16[256,256]{1,0:T(8,128)(2,1)}) custom-call(bf16[192,256]{1,0:T(8,128)(2,1)S(1)} %get-tuple-element.15.refs_0_, bf16[256,256]{1,0:T(8,128)(2,1)S(1)} %get-tuple-element.16.refs_1_, ...), custom_call_target="tpu_custom_call" | custom-call | tf_op jit(solution)/shard_map/store/pallas_call | solution.py:757

commit v14 on v13

--- a/solution.py
+++ b/solution.py
@@ -335,11 +335,11 @@
     lax.fori_loop(0, Z, w_near, 0)
 
     arrived(bsib, b_recv)
-    scan_send(0)
     bchip[y] = bown[...] + bsib[...]
     for distance in range(1, Y):
         place = lax.rem(y + distance, Y)
         send(bchip.at[y], bchip.at[y], bc_send, bc_recv.at[distance - 1], at_y(place))
+    scan_send(0)
 
     for load in loads[3:]:
         load.wait()

time: 80.3 us -> 78.8 us (0.981)
  Pallas kernels: 78.9 us -> 78 us
    pallas_call x1, Pallas kernels: 78.1 us -> 77.2 us  [on_device(): pl.pallas_call(functools.partial(kernel, chips), out_shape=tuple((pltpu.V...]
where the time goes in v14:
time: 78.8 us; the launch traced here: 78.7 us
  Pallas kernels  78 us (99%)
    pallas_call x1, Pallas kernels, on_device(): pl.pallas_call(functools.partial(kernel, chips), out_shape=tuple((pltpu.V...  77.2 us

profile of v14, /device:TPU:1, one launch (start us, length us, event | category | flops | bytes accessed | tf_op | source)
XLA Modules:
  0.0 78.7 jit_solution(9304247678084269950)
XLA Ops:
  0.6 77.2 %attention_layer.1 = (bf16[192,256]{1,0:T(8,128)(2,1)S(1)}, bf16[256,256]{1,0:T(8,128)(2,1)S(1)}, bf16[256,256]{1,0:T(8,128)(2,1)S(1)}, bf16[256,256]{1,0:T(8,128)(2,1)S(1)}, bf16[256,256]{1,0:T(8,128)(2,1)S(1)}) custom-call(bf16[256,256]{1,0:T(8,128)(2,1)} %q_in.1, bf16[256,256]{1,0:T(8,128)(2,1)} %k_in.1, bf16[256,256]{1,0:T(8,128)(2,1)} %v_in.1, ...), custom_call_target="tpu_custom_call" | custom-call | flops 2000000000 | bytes 8000000 | tf_op jit(solution)/shard_map/attention_layer/pallas_call | solution.py:745
  77.8 0.9 %store.1 = (bf16[192,256]{1,0:T(8,128)(2,1)}, bf16[256,256]{1,0:T(8,128)(2,1)}, bf16[256,256]{1,0:T(8,128)(2,1)}, bf16[256,256]{1,0:T(8,128)(2,1)}, bf16[256,256]{1,0:T(8,128)(2,1)}) custom-call(bf16[192,256]{1,0:T(8,128)(2,1)S(1)} %get-tuple-element.15.refs_0_, bf16[256,256]{1,0:T(8,128)(2,1)S(1)} %get-tuple-element.16.refs_1_, ...), custom_call_target="tpu_custom_call" | custom-call | tf_op jit(solution)/shard_map/store/pallas_call | solution.py:757
